TPU v7x, 32 devices: a whole 2x2x4 slice. The times are simulated.
32 devices in a mesh: ctx: 8 (over y, x, core), fsdp: 4 (over z).
Axes of the slice: x: 2, y: 2, z: 4, core: 2. Of those that a mesh axis runs over, the one named last changes fastest.
Arguments:
- tokens: bfloat16 [16, 256, 2048], P('ctx', 'fsdp'), may hold values from -6 to 6
- block_order: int32 [16], replicated, may hold values from 0 to 15, as said below
- w_query: bfloat16 [2048, 2048], P('fsdp'), may hold values from -0.125 to 0.125
- w_key: bfloat16 [2048, 2048], P('fsdp'), may hold values from -0.125 to 0.125
- w_value: bfloat16 [2048, 2048], P('fsdp'), may hold values from -0.125 to 0.125
- w_out: bfloat16 [2048, 2048], P('fsdp'), may hold values from -1 to 1
- w_gate: bfloat16 [2048, 8192], P('fsdp'), may hold values from -0.125 to 0.125
- w_up: bfloat16 [2048, 8192], P('fsdp'), may hold values from -0.125 to 0.125
- w_down: bfloat16 [2048, 8192], P('fsdp'), may hold values from -0.0625 to 0.0625
- gain_attn: bfloat16 [2048], P('fsdp'), may hold values from 0.099609375 to 1.8984375
- gain_mlp: bfloat16 [2048], P('fsdp'), may hold values from 0.099609375 to 1.8984375
- cotangent: bfloat16 [16, 256, 2048], P('ctx', 'fsdp'), may hold values from -6 to 6
Outputs:
- result: bfloat16 [16, 256, 2048], P('ctx', 'fsdp')
- grad_tokens: float32 [16, 256, 2048], P('ctx', 'fsdp')
- grad_w_query: float32 [2048, 2048], P(('ctx', 'fsdp'))
- grad_w_key: float32 [2048, 2048], P(('ctx', 'fsdp'))
- grad_w_value: float32 [2048, 2048], P(('ctx', 'fsdp'))
- grad_w_out: float32 [2048, 2048], P(('ctx', 'fsdp'))
- grad_w_gate: float32 [2048, 8192], P(('ctx', 'fsdp'))
- grad_w_up: float32 [2048, 8192], P(('ctx', 'fsdp'))
- grad_w_down: float32 [2048, 8192], P(('ctx', 'fsdp'))
- grad_gain_attn: float32 [2048], P(('ctx', 'fsdp'))
- grad_gain_mlp: float32 [2048], P(('ctx', 'fsdp'))
Inputs may be any that keep to these rules, and one draw needn't show every extreme that they name: `block_order`: A permutation of the 16 sequence blocks. Slots 2 c and 2 c + 1 (the two slots of one device along ctx) hold blocks k and 15 - k for some k.
All inputs are finite; a program needn't handle non-finite values.
Results may differ from a plain program's by a relative error of at most 0.022.
Values may be sent and summed in bfloat16 or wider, within the bound.
No kernel may reach another device: no remote copies, remote signals or barrier semaphores. Data moves between devices by JAX's collectives and lax.ppermute only.
A program may use at most 320 MiB of HBM per device.

v0:
```python
import functools

import jax
import jax.numpy as jnp
from jax import lax
from jax.experimental import pallas as pl
from jax.experimental.pallas import tpu as pltpu
from jax.sharding import PartitionSpec as P

HEAD_DIM = 64


EPSILON = 1e-05
ROPE_BASE = 130000.0
MASKED_SCORE = -1e30


def rotate(values, places, direction):
    half_dim = values.shape[-1] // 2
    frequency = 1.0 / ROPE_BASE ** (
        jnp.arange(half_dim, dtype=jnp.float32) * (2.0 / values.shape[-1])
    )
    angles = places[..., None] * frequency
    cosine = jnp.cos(angles)[..., None, :]
    sine_part = direction * jnp.sin(angles)[..., None, :]
    leading = values[..., :half_dim]
    trailing = values[..., half_dim:]
    return jnp.concatenate(
        [leading * cosine - trailing * sine_part, trailing * cosine + leading * sine_part], -1
    )


def matmul(left, right):
    return jnp.dot(left, right, preferred_element_type=jnp.float32)


def contract(left, right):
    return lax.dot_general(
        left, right, (((1,), (1,)), ((), ())), preferred_element_type=jnp.float32
    )


def transpose_product(left, right):
    return lax.dot_general(
        left, right, (((0,), (0,)), ((), ())), preferred_element_type=jnp.float32
    )


def split_heads(values):
    return values.reshape(values.shape[:-1] + (-1, HEAD_DIM))


def keep_state(current):
    return current


def tile_scores(queries, key_rows, query_places, key_places, score_scale):
    scores = (
        jnp.einsum("qhd,khd->hqk", queries, key_rows, preferred_element_type=jnp.float32)
        * score_scale
    )
    allowed = (key_places[None, :] <= query_places[:, None])[None]
    return (jnp.where(allowed, scores, MASKED_SCORE), allowed)


def grow_state(current, queries, key_rows, value_rows, query_places, key_places, score_scale):
    run_peak, run_total, summed = current
    scores, allowed = tile_scores(queries, key_rows, query_places, key_places, score_scale)
    new_peak = jnp.maximum(run_peak, jnp.max(scores, -1))
    weights = jnp.where(allowed, jnp.exp(scores - new_peak[..., None]), 0.0)
    factor = jnp.exp(run_peak - new_peak)
    run_total = run_total * factor + jnp.sum(weights, -1)
    summed = summed * jnp.transpose(factor)[:, :, None] + jnp.einsum(
        "hqk,khd->qhd", weights.astype(jnp.bfloat16), value_rows, preferred_element_type=jnp.float32
    )
    return (new_peak, run_total, summed)


def backward_tile(
    queries,
    key_rows,
    value_rows,
    grad_out,
    log_total,
    row_delta,
    query_places,
    key_places,
    score_scale,
):
    scores, allowed = tile_scores(queries, key_rows, query_places, key_places, score_scale)
    probabilities = jnp.where(allowed, jnp.exp(scores - log_total[..., None]), 0.0)
    grad_probs = jnp.einsum(
        "qhd,khd->hqk", grad_out, value_rows, preferred_element_type=jnp.float32
    )
    grad_scores = (probabilities * (grad_probs - row_delta[..., None])).astype(jnp.bfloat16)
    return (probabilities, grad_scores)


def norm_back(grad_normed_in, normed_values, inverse_root, gain_vector):
    scaled = grad_normed_in * gain_vector
    return inverse_root * (
        scaled - normed_values * jnp.mean(scaled * normed_values, -1, keepdims=True)
    )


def per_device(
    tokens,
    block_order,
    w_query,
    w_key,
    w_value,
    w_out,
    w_gate,
    w_up,
    w_down,
    gain_attn,
    gain_mlp,
    cotangent,
):
    slot_count, share_rows, model_width = tokens.shape
    fsdp_size = lax.axis_size("fsdp")
    block_rows = share_rows * fsdp_size
    head_width = model_width // fsdp_size
    heads_here = head_width // HEAD_DIM
    row_count = slot_count * share_rows
    score_scale = HEAD_DIM ** (-0.5)
    own_slots = 2 * lax.axis_index("ctx") + jnp.arange(2, dtype=jnp.int32)
    own_blocks = block_order[own_slots]
    token_places = (
        (
            own_blocks[:, None] * block_rows
            + lax.axis_index("fsdp") * share_rows
            + jnp.arange(share_rows, dtype=jnp.int32)[None, :]
        )
        .astype(jnp.float32)
        .reshape(row_count)
    )
    head_places = (
        own_blocks[:, None] * block_rows + jnp.arange(block_rows, dtype=jnp.int32)[None, :]
    ).astype(jnp.float32)
    params = (w_query, w_key, w_value, w_out, w_gate, w_up, w_down, gain_attn, gain_mlp)
    weights_all = (
        lax.all_gather(params[0], "fsdp", axis=0, tiled=True),
        lax.all_gather(params[1], "fsdp", axis=0, tiled=True),
        lax.all_gather(params[2], "fsdp", axis=0, tiled=True),
        lax.all_gather(params[3], "fsdp", axis=0, tiled=True),
        lax.all_gather(params[4], "fsdp", axis=0, tiled=True),
        lax.all_gather(params[5], "fsdp", axis=0, tiled=True),
        lax.all_gather(params[6], "fsdp", axis=0, tiled=True),
        lax.all_gather(params[7], "fsdp", axis=0, tiled=True),
        lax.all_gather(params[8], "fsdp", axis=0, tiled=True),
    )
    stream = tokens.reshape(row_count, model_width).astype(jnp.float32)
    root_one = lax.rsqrt(jnp.mean(stream * stream, -1, keepdims=True) + EPSILON)
    norm_one = stream * root_one
    attn_input = (norm_one * weights_all[7].astype(jnp.float32)).astype(jnp.bfloat16)

    def project_turn(weight):
        linear = matmul(attn_input, weight).reshape(row_count, -1, HEAD_DIM)
        return (
            rotate(linear, token_places, 1.0)
            .astype(jnp.bfloat16)
            .reshape(slot_count, share_rows, model_width)
        )

    query_tok = project_turn(weights_all[0])
    key_tok = project_turn(weights_all[1])
    value_tok = (
        matmul(attn_input, weights_all[2])
        .astype(jnp.bfloat16)
        .reshape(slot_count, share_rows, model_width)
    )
    query_heads, key_heads, value_heads = (
        lax.all_to_all(query_tok, "fsdp", split_axis=2, concat_axis=1, tiled=True),
        lax.all_to_all(key_tok, "fsdp", split_axis=2, concat_axis=1, tiled=True),
        lax.all_to_all(value_tok, "fsdp", split_axis=2, concat_axis=1, tiled=True),
    )
    query_split = split_heads(query_heads)
    start_state = tuple(
        (
            (
                jnp.full((heads_here, block_rows), MASKED_SCORE, jnp.float32),
                jnp.zeros((heads_here, block_rows), jnp.float32),
                jnp.zeros((block_rows, heads_here, HEAD_DIM), jnp.float32),
            )
            for which_slot in range(2)
        )
    )
    carried = start_state
    key_part = lax.all_gather(key_heads, "ctx", axis=0, tiled=True)
    value_part = lax.all_gather(value_heads, "ctx", axis=0, tiled=True)

    def visit_slot(inner_state, element):
        key_one, value_one, offset = element
        key_block = block_order[offset]
        key_places = (key_block * block_rows + jnp.arange(block_rows, dtype=jnp.int32)).astype(
            jnp.float32
        )
        key_split = split_heads(key_one)
        value_split = split_heads(value_one)
        updated = []
        for which_slot in range(2):

            def grow_one(current, which_slot=which_slot):
                return grow_state(
                    current,
                    query_split[which_slot],
                    key_split,
                    value_split,
                    head_places[which_slot],
                    key_places,
                    score_scale,
                )

            updated.append(
                lax.cond(
                    key_block <= own_blocks[which_slot],
                    grow_one,
                    keep_state,
                    inner_state[which_slot],
                )
            )
        return (tuple(updated), None)

    offsets = jnp.arange(key_part.shape[0], dtype=jnp.int32)
    carried, unused = lax.scan(visit_slot, carried, (key_part, value_part, offsets))
    attended_parts = []
    log_parts = []
    for which_slot in range(2):
        run_peak, run_total, summed = carried[which_slot]
        log_parts.append(run_peak + jnp.log(run_total))
        attended_parts.append(summed / jnp.transpose(run_total)[:, :, None])
    attended = jnp.stack(attended_parts)
    log_total = jnp.stack(log_parts)
    mixed_send = attended.reshape(slot_count, block_rows, head_width).astype(jnp.bfloat16)
    mixed_tok = lax.all_to_all(mixed_send, "fsdp", split_axis=1, concat_axis=2, tiled=True)
    mixed_flat = mixed_tok.reshape(row_count, model_width)
    middle = stream + matmul(mixed_flat, weights_all[3])
    root_two = lax.rsqrt(jnp.mean(middle * middle, -1, keepdims=True) + EPSILON)
    norm_two = middle * root_two
    mlp_input = (norm_two * weights_all[8].astype(jnp.float32)).astype(jnp.bfloat16)
    gate_act = matmul(mlp_input, weights_all[4])
    upward = matmul(mlp_input, weights_all[5])
    gate_sigmoid = jax.nn.sigmoid(gate_act)
    gate_silu = gate_act * gate_sigmoid
    hidden = (gate_silu * upward).astype(jnp.bfloat16)
    output = middle + contract(hidden, weights_all[6])
    result = output.astype(jnp.bfloat16).reshape(slot_count, share_rows, model_width)
    upstream = cotangent.reshape(row_count, model_width)
    grad_hidden = matmul(upstream, weights_all[6])
    grad_gate = (
        grad_hidden * upward * gate_sigmoid * (1.0 + gate_act * (1.0 - gate_sigmoid))
    ).astype(jnp.bfloat16)
    grad_up = (grad_hidden * gate_silu).astype(jnp.bfloat16)
    grad_two = contract(grad_gate, weights_all[4]) + contract(grad_up, weights_all[5])
    gain_two_part = jnp.sum(grad_two * norm_two, 0)
    grad_middle = upstream.astype(jnp.float32) + norm_back(
        grad_two, norm_two, root_two, weights_all[8].astype(jnp.float32)
    )
    grad_branch = grad_middle.astype(jnp.bfloat16)
    grad_mixed = (
        contract(grad_branch, weights_all[3])
        .astype(jnp.bfloat16)
        .reshape(slot_count, share_rows, model_width)
    )
    grad_heads = lax.all_to_all(grad_mixed, "fsdp", split_axis=2, concat_axis=1, tiled=True)
    grad_split = split_heads(grad_heads)
    row_delta = jnp.transpose(jnp.sum(grad_split.astype(jnp.float32) * attended, -1), (0, 2, 1))
    gathered = (
        lax.all_gather(key_heads, "ctx", axis=0, tiled=True),
        lax.all_gather(value_heads, "ctx", axis=0, tiled=True),
    )
    key_all, value_all = gathered
    total_slots = key_all.shape[0]

    def query_visit(current, element):
        key_pair, value_pair, pair_index = element
        updated = list(current)
        for member in range(2):
            key_block = block_order[2 * pair_index + member]
            key_places = (key_block * block_rows + jnp.arange(block_rows, dtype=jnp.int32)).astype(
                jnp.float32
            )
            key_split = split_heads(key_pair[member])
            value_split = split_heads(value_pair[member])
            for which_slot in range(2):

                def take_query(
                    accum,
                    which_slot=which_slot,
                    key_split=key_split,
                    value_split=value_split,
                    key_places=key_places,
                ):
                    probabilities, grad_scores = backward_tile(
                        query_split[which_slot],
                        key_split,
                        value_split,
                        grad_split[which_slot],
                        log_total[which_slot],
                        row_delta[which_slot],
                        head_places[which_slot],
                        key_places,
                        score_scale,
                    )
                    return accum + score_scale * jnp.einsum(
                        "hqk,khd->qhd", grad_scores, key_split, preferred_element_type=jnp.float32
                    )

                updated[which_slot] = lax.cond(
                    key_block <= own_blocks[which_slot], take_query, keep_state, updated[which_slot]
                )
        return (tuple(updated), None)

    query_zero = jnp.zeros((block_rows, heads_here, HEAD_DIM), jnp.float32)
    pair_keys = key_all.reshape(total_slots // 2, 2, block_rows, head_width)
    pair_values = value_all.reshape(total_slots // 2, 2, block_rows, head_width)
    grad_query_parts, unused = lax.scan(
        query_visit,
        (query_zero, query_zero),
        (pair_keys, pair_values, jnp.arange(total_slots // 2, dtype=jnp.int32)),
    )
    key_part = key_all
    value_part = value_all

    def key_visit(unused_carry, element):
        key_one, value_one, offset = element
        key_block = block_order[offset]
        key_places = (key_block * block_rows + jnp.arange(block_rows, dtype=jnp.int32)).astype(
            jnp.float32
        )
        key_split = split_heads(key_one)
        value_split = split_heads(value_one)
        sums = (
            jnp.zeros((block_rows, heads_here, HEAD_DIM), jnp.float32),
            jnp.zeros((block_rows, heads_here, HEAD_DIM), jnp.float32),
        )
        for which_slot in range(2):

            def take_keys(current, which_slot=which_slot):
                probabilities, grad_scores = backward_tile(
                    query_split[which_slot],
                    key_split,
                    value_split,
                    grad_split[which_slot],
                    log_total[which_slot],
                    row_delta[which_slot],
                    head_places[which_slot],
                    key_places,
                    score_scale,
                )
                grad_key = current[0] + score_scale * jnp.einsum(
                    "hqk,qhd->khd",
                    grad_scores,
                    query_split[which_slot],
                    preferred_element_type=jnp.float32,
                )
                grad_value = current[1] + jnp.einsum(
                    "hqk,qhd->khd",
                    probabilities.astype(jnp.bfloat16),
                    grad_split[which_slot],
                    preferred_element_type=jnp.float32,
                )
                return (grad_key, grad_value)

            sums = lax.cond(key_block <= own_blocks[which_slot], take_keys, keep_state, sums)
        joined = jnp.concatenate(
            [sums[0].reshape(block_rows, head_width), sums[1].reshape(block_rows, head_width)], -1
        )
        return (unused_carry, joined)

    unused_final, terms = lax.scan(
        key_visit,
        jnp.zeros((), jnp.float32),
        (key_part, value_part, jnp.arange(slot_count * lax.axis_size("ctx"), dtype=jnp.int32)),
    )
    summed_kv = lax.psum_scatter(
        terms.astype(jnp.bfloat16), "ctx", scatter_dimension=0, tiled=True
    ).astype(jnp.float32)
    grad_keys = (
        rotate(split_heads(summed_kv[..., :head_width]), head_places, -1.0)
        .astype(jnp.bfloat16)
        .reshape(slot_count, block_rows, head_width)
    )
    grad_values = summed_kv[..., head_width:].astype(jnp.bfloat16)
    grad_queries = (
        rotate(jnp.stack(grad_query_parts), head_places, -1.0)
        .astype(jnp.bfloat16)
        .reshape(slot_count, block_rows, head_width)
    )
    grad_q_tok, grad_k_tok, grad_v_tok = (
        lax.all_to_all(grad_queries, "fsdp", split_axis=1, concat_axis=2, tiled=True),
        lax.all_to_all(grad_keys, "fsdp", split_axis=1, concat_axis=2, tiled=True),
        lax.all_to_all(grad_values, "fsdp", split_axis=1, concat_axis=2, tiled=True),
    )
    grad_q_lin = grad_q_tok.reshape(row_count, model_width)
    grad_k_lin = grad_k_tok.reshape(row_count, model_width)
    grad_v_lin = grad_v_tok.reshape(row_count, model_width)
    grad_one = (
        contract(grad_q_lin, weights_all[0])
        + contract(grad_k_lin, weights_all[1])
        + contract(grad_v_lin, weights_all[2])
    )
    gain_one_part = jnp.sum(grad_one * norm_one, 0)
    grad_input = grad_middle + norm_back(
        grad_one, norm_one, root_one, weights_all[7].astype(jnp.float32)
    )
    hidden_width = hidden.shape[1]
    gain_parts = jnp.stack([gain_one_part, gain_two_part], 1)
    wide_cols = (
        lax.all_to_all(grad_q_lin, "fsdp", split_axis=1, concat_axis=0, tiled=True),
        lax.all_to_all(grad_k_lin, "fsdp", split_axis=1, concat_axis=0, tiled=True),
        lax.all_to_all(grad_v_lin, "fsdp", split_axis=1, concat_axis=0, tiled=True),
        lax.all_to_all(grad_branch, "fsdp", split_axis=1, concat_axis=0, tiled=True),
        lax.all_to_all(grad_gate, "fsdp", split_axis=1, concat_axis=0, tiled=True),
        lax.all_to_all(grad_up, "fsdp", split_axis=1, concat_axis=0, tiled=True),
        lax.all_to_all(hidden, "fsdp", split_axis=1, concat_axis=0, tiled=True),
    )
    row_sets = (
        lax.all_gather(attn_input, "fsdp", axis=0, tiled=True),
        lax.all_gather(mixed_flat, "fsdp", axis=0, tiled=True),
        lax.all_gather(mlp_input, "fsdp", axis=0, tiled=True),
        lax.all_gather(upstream, "fsdp", axis=0, tiled=True),
    )
    group_rows = model_width // lax.axis_size("ctx")
    row_cuts = [values for values in row_sets]
    pieces = [
        transpose_product(row_cuts[0], wide_cols[0]),
        transpose_product(row_cuts[0], wide_cols[1]),
        transpose_product(row_cuts[0], wide_cols[2]),
        transpose_product(row_cuts[1], wide_cols[3]),
        transpose_product(row_cuts[2], wide_cols[4]),
        transpose_product(row_cuts[2], wide_cols[5]),
        transpose_product(row_cuts[3], wide_cols[6]),
        gain_parts,
        jnp.zeros((group_rows * lax.axis_size("ctx"), 126), jnp.float32),
    ]
    partial_sums = lax.psum_scatter(
        jnp.concatenate(pieces, 1).astype(jnp.bfloat16), "ctx", scatter_dimension=0, tiled=True
    ).astype(jnp.float32)
    owned = lax.all_to_all(
        partial_sums.astype(jnp.bfloat16), "fsdp", split_axis=0, concat_axis=1, tiled=True
    ).astype(partial_sums.dtype)
    span_width = partial_sums.shape[1]
    owned_rows = owned.shape[0]
    arranged = owned.reshape(owned_rows, fsdp_size, span_width)
    model_part = model_width // fsdp_size
    hidden_part = hidden_width // fsdp_size
    bounds = [
        0,
        model_part,
        2 * model_part,
        3 * model_part,
        4 * model_part,
        4 * model_part + hidden_part,
        4 * model_part + 2 * hidden_part,
        4 * model_part + 3 * hidden_part,
    ]

    def joined_cols(first_col, last_col):
        return arranged[:, :, first_col:last_col].reshape(owned_rows, -1)

    grad_w_query = joined_cols(bounds[0], bounds[1])
    grad_w_key = joined_cols(bounds[1], bounds[2])
    grad_w_value = joined_cols(bounds[2], bounds[3])
    grad_w_out = joined_cols(bounds[3], bounds[4])
    grad_w_gate = joined_cols(bounds[4], bounds[5])
    grad_w_up = joined_cols(bounds[5], bounds[6])
    grad_w_down = joined_cols(bounds[6], bounds[7])
    gain_totals = jnp.sum(arranged[:, :, bounds[7] : bounds[7] + 2], 1)
    grad_gain_attn = gain_totals[:, 0]
    grad_gain_mlp = gain_totals[:, 1]
    grad_tokens = grad_input.reshape(slot_count, share_rows, model_width)
    return (
        result,
        grad_tokens,
        grad_w_query,
        grad_w_key,
        grad_w_value,
        grad_w_out,
        grad_w_gate,
        grad_w_up,
        grad_w_down,
        grad_gain_attn,
        grad_gain_mlp,
    )


def dot_f32(a, b):
    return jnp.dot(a, b, preferred_element_type=jnp.float32)

def load_sequence(order_ref, rows_ref, block, stores):
    per_src = rows_ref.shape[2] // block
    def one(slot, carry):
        src = slot // per_src
        lane = pl.multiple_of((slot % per_src) * block, block)
        place = pl.multiple_of(order_ref[slot] * block, block)
        for at, store in stores:
            store(rows_ref[src, at:at + HEAD_DIM, pl.ds(lane, block)], place)
        return carry
    lax.fori_loop(0, rows_ref.shape[0] * per_src, one, 0)

def fwd_kernel(
    order_ref, qkv_ref, mixed_ref, out_ref, lse_ref, qt, kr, vt, peak, total, acc, *, block, tile, step
):
    seq = qt.shape[1]

    def put_q(x, place):
        qt[:, pl.ds(place, block)] = x * jnp.bfloat16(HEAD_DIM ** -0.5)

    def put_k(x, place):
        kr[pl.ds(place, block), :] = x.T

    def put_v(x, place):
        vt[:, pl.ds(place, block)] = x

    load_sequence(
        order_ref, qkv_ref, block, ((0, put_q), (HEAD_DIM, put_k), (2 * HEAD_DIM, put_v))
    )

    def one_tile(qi, unused):
        q0 = pl.multiple_of(qi * tile, tile)
        peak[...] = jnp.full_like(peak, MASKED_SCORE)
        total[...] = jnp.zeros_like(total)
        acc[...] = jnp.zeros_like(acc)

        def visit(k0, first, masked):
            queries = qt[:, pl.ds(pl.multiple_of(q0 + first, step), tile - first)]
            s = dot_f32(kr[pl.ds(k0, step), :], queries)
            if masked:
                keep = lax.broadcasted_iota(jnp.int32, s.shape, 0) <= lax.broadcasted_iota(
                    jnp.int32, s.shape, 1
                )
                s = jnp.where(keep, s, MASKED_SCORE)
            old = peak[:, first:]
            new = jnp.maximum(old, jnp.max(s, 0, keepdims=True))
            p = jnp.exp(s - new)
            alpha = jnp.exp(old - new)
            peak[:, first:] = new
            total[:, first:] = total[:, first:] * alpha + jnp.sum(p, 0, keepdims=True)
            acc[:, first:] = acc[:, first:] * alpha + dot_f32(
                vt[:, pl.ds(k0, step)], p.astype(jnp.bfloat16)
            )

        def below(j, carry):
            visit(pl.multiple_of(j * step, step), 0, False)
            return carry

        lax.fori_loop(0, qi * (tile // step), below, 0)
        for part in range(tile // step):
            visit(pl.multiple_of(q0 + part * step, step), part * step, True)
        out_ref[:, pl.ds(q0, tile)] = acc[...] / total[...]
        lse_ref[:, pl.ds(q0, tile)] = peak[...] + jnp.log(total[...])
        return unused

    lax.fori_loop(0, seq // tile, one_tile, 0)
    per_src = mixed_ref.shape[2] // block

    def send(slot, carry):
        place = pl.multiple_of(order_ref[slot] * block, block)
        lane = pl.multiple_of((slot % per_src) * block, block)
        mixed_ref[slot // per_src, :, pl.ds(lane, block)] = out_ref[:, pl.ds(place, block)].astype(
            jnp.bfloat16
        )
        return carry

    lax.fori_loop(0, mixed_ref.shape[0] * per_src, send, 0)


def attend(order, qkv, block, tile, step):
    groups, unused, width = qkv.shape
    seq = groups * width
    vm = pl.BlockSpec(memory_space=pltpu.VMEM)
    bf, f32 = jnp.bfloat16, jnp.float32
    return pl.pallas_call(
        functools.partial(fwd_kernel, block=block, tile=tile, step=step),
        out_shape=(
            jax.ShapeDtypeStruct((groups, HEAD_DIM, width), bf),
            jax.ShapeDtypeStruct((HEAD_DIM, seq), f32),
            jax.ShapeDtypeStruct((1, seq), f32),
        ),
        in_specs=[pl.BlockSpec(memory_space=pltpu.SMEM), vm],
        out_specs=(vm, vm, vm),
        scratch_shapes=[
            pltpu.VMEM((HEAD_DIM, seq), bf),
            pltpu.VMEM((seq, HEAD_DIM), bf),
            pltpu.VMEM((HEAD_DIM, seq), bf),
            pltpu.VMEM((1, tile), f32),
            pltpu.VMEM((1, tile), f32),
            pltpu.VMEM((HEAD_DIM, tile), f32),
        ],
        compiler_params=pltpu.CompilerParams(vmem_limit_bytes=48 << 20),
        cost_estimate=pl.CostEstimate(
            flops=int(4.0 * seq * seq * HEAD_DIM),
            bytes_accessed=8 * seq * HEAD_DIM,
            transcendentals=0,
        ),
        name="attend",
    )(order, qkv)


def bwd_kernel(order_ref, qkv_ref, go_ref, out_ref, lse_ref, cos_ref, sin_ref, grad_ref,
               qt, qr, kt, kr, vr, got, gor, delta, dqt, dkr, dvr, *, block, tile, step):
    seq = qt.shape[1]
    scale = jnp.bfloat16(HEAD_DIM ** -0.5)
    def put_q(x, place):
        x = x * scale
        qt[:, pl.ds(place, block)] = x
        qr[pl.ds(place, block), :] = x.T
    def put_k(x, place):
        kt[:, pl.ds(place, block)] = x * scale
        kr[pl.ds(place, block), :] = x.T
    def put_v(x, place):
        vr[pl.ds(place, block), :] = x.T
    def put_go(x, place):
        got[:, pl.ds(place, block)] = x
        gor[pl.ds(place, block), :] = x.T
        delta[:, pl.ds(place, block)] = jnp.sum(x.astype(jnp.float32) * out_ref[:, pl.ds(place, block)], 0, keepdims=True)
    load_sequence(order_ref, qkv_ref, block, ((0, put_q), (HEAD_DIM, put_k), (2 * HEAD_DIM, put_v)))
    load_sequence(order_ref, go_ref, block, ((0, put_go),))
    dqt[...] = jnp.zeros_like(dqt)
    tiles = seq // tile

    def key_tile(kj, unused):
        k0 = pl.multiple_of(kj * tile, tile)
        keys = kr[pl.ds(k0, tile), :]
        keys_t = kt[:, pl.ds(k0, tile)]
        vals = vr[pl.ds(k0, tile), :]
        dkr[...] = jnp.zeros_like(dkr)
        dvr[...] = jnp.zeros_like(dvr)

        def visit(q0, width, rows, masked):
            s = dot_f32(keys[:rows], qt[:, pl.ds(q0, width)])
            p = jnp.exp(s - lse_ref[:, pl.ds(q0, width)])
            if masked:
                keep = lax.broadcasted_iota(jnp.int32, s.shape, 0) <= lax.broadcasted_iota(
                    jnp.int32, s.shape, 1
                ) + (rows - width)
                p = jnp.where(keep, p, 0.0)
            dp = dot_f32(vals[:rows], got[:, pl.ds(q0, width)])
            ds = (p * (dp - delta[:, pl.ds(q0, width)])).astype(jnp.bfloat16)
            dvr[:rows] += dot_f32(p.astype(jnp.bfloat16), gor[pl.ds(q0, width), :])
            dkr[:rows] += dot_f32(ds, qr[pl.ds(q0, width), :])
            dqt[:, pl.ds(q0, width)] += dot_f32(keys_t[:, :rows], ds)

        for part in range(tile // step):
            first = pl.multiple_of(k0 + part * step, step)
            visit(first, step, (part + 1) * step, True)

        def later(j, carry):
            visit(pl.multiple_of(j * step, step), step, tile, False)
            return carry

        lax.fori_loop((kj + 1) * (tile // step), seq // step, later, 0)
        put_out(dkr[...].T, HEAD_DIM, k0, True)
        put_out(dvr[...].T, 2 * HEAD_DIM, k0, False)
        return unused

    half = HEAD_DIM // 2
    def put_out(x, at, place, turn):
        for part in range(tile // block):
            piece = x[:, part * block:(part + 1) * block]
            here = place + part * block
            if turn:
                lanes = pl.ds(pl.multiple_of(here, block), block)
                c, s = cos_ref[:, lanes], sin_ref[:, lanes]
                a, b = piece[:half], piece[half:]
                piece = jnp.concatenate([a * c + b * s, b * c - a * s], 0)
            slot = order_ref[seq // block + here // block]
            per_src = grad_ref.shape[2] // block
            lane = pl.multiple_of((slot % per_src) * block, block)
            grad_ref[slot // per_src, at:at + HEAD_DIM, pl.ds(lane, block)] = piece.astype(jnp.bfloat16)

    lax.fori_loop(0, tiles, key_tile, 0)
    def write_q(qi, c):
        q0 = pl.multiple_of(qi * tile, tile)
        put_out(dqt[:, pl.ds(q0, tile)], 0, q0, True)
        return c
    lax.fori_loop(0, tiles, write_q, 0)

def attend_back(order, qkv, go, out, lse, cos, sin, block, tile, step):
    groups, unused, width = qkv.shape
    seq = groups * width
    vm = pl.BlockSpec(memory_space=pltpu.VMEM)
    bf, f32 = jnp.bfloat16, jnp.float32
    wide = lambda t: pltpu.VMEM((HEAD_DIM, seq), t)
    tall = lambda t: pltpu.VMEM((seq, HEAD_DIM), t)
    return pl.pallas_call(
        functools.partial(bwd_kernel, block=block, tile=tile, step=step),
        out_shape=jax.ShapeDtypeStruct(qkv.shape, bf),
        in_specs=[pl.BlockSpec(memory_space=pltpu.SMEM)] + [vm] * 6,
        out_specs=vm,
        scratch_shapes=[wide(bf), tall(bf), wide(bf), tall(bf), tall(bf), wide(bf), tall(bf),
                        pltpu.VMEM((1, seq), f32), wide(f32),
                        pltpu.VMEM((tile, HEAD_DIM), f32), pltpu.VMEM((tile, HEAD_DIM), f32)],
        compiler_params=pltpu.CompilerParams(vmem_limit_bytes=48 << 20),
        cost_estimate=pl.CostEstimate(
            flops=int(6.4 * seq * seq * HEAD_DIM),
            bytes_accessed=16 * seq * HEAD_DIM,
            transcendentals=0,
        ),
        name="attend_back",
    )(order, qkv, go, out, lse, cos, sin)


def nt_dot(a, b):
    return lax.dot_general(a, b, (((1,), (1,)), ((), ())), preferred_element_type=jnp.float32)


def whole(space=pltpu.VMEM):
    return pl.BlockSpec(memory_space=space)


def spread(pieces, place_ref, rows_ref):
    hops = (len(pieces) - 1) // 2
    slots, share, unused = pieces[0].shape
    place = place_ref[0]

    def put(piece, position):
        for slot in range(slots):
            first = pl.multiple_of(slot * share * (hops + 1) + position * share, share)
            rows_ref[pl.ds(first, share), :] = piece[slot]

    put(pieces[0], place)
    for hop in range(1, hops + 1):

        @pl.when(place >= hop)
        def take_below(hop=hop):
            put(pieces[hop], place - hop)

        @pl.when(place + hop <= hops)
        def take_above(hop=hop):
            put(pieces[hops + hop], place + hop)


def deal(rows_ref, place_ref, own_ref, others):
    slots, share, unused = own_ref.shape
    line = len(others) + 1
    for step, target in enumerate([own_ref] + list(others)):
        position = lax.rem(place_ref[0] + step, line)
        for slot in range(slots):
            first = pl.multiple_of(slot * share * line + position * share, share)
            target[slot] = rows_ref[pl.ds(first, share), :].astype(target.dtype)


def dealt_shapes(slots, share, width, line):
    return [jax.ShapeDtypeStruct((slots, share, width), jnp.float32)] + [
        jax.ShapeDtypeStruct((slots, share, width), jnp.bfloat16) for unused in range(line - 1)
    ]


def work(flops, bytes_accessed=0, transcendentals=0):
    return pl.CostEstimate(
        flops=int(flops * 0.2), bytes_accessed=int(bytes_accessed * 0.2), transcendentals=0
    )


def vmem_limit(mebibytes):
    return pltpu.CompilerParams(vmem_limit_bytes=mebibytes << 20)


EXTRA_ROWS = 16
LANES = 128


def cut_columns(place, group, weights, rows, line, extra=None):
    count = len(weights)
    columns = weights[0].shape[1] // line
    cut_rows = count * rows + (EXTRA_ROWS if extra is not None else 0)
    extras = [] if extra is None else [extra]

    def kernel(place_ref, group_ref, *refs):
        outs = refs[count * line + len(extras) :]
        for step in range(line):
            for i in range(count):
                outs[step][i * rows : (i + 1) * rows] = refs[step * count + i][...]
            if extras:
                outs[step][count * rows :] = refs[count * line][...]

    def target(step):
        return lambda i, place, group: (group[0], lax.rem(place[0] + step, line))

    fixed = lambda shape: pl.BlockSpec(shape, lambda i, place, group: (0, 0))
    return pl.pallas_call(
        kernel,
        out_shape=[jax.ShapeDtypeStruct((cut_rows, columns), jnp.bfloat16)] * line,
        grid_spec=pltpu.PrefetchScalarGridSpec(
            num_scalar_prefetch=2,
            grid=(1,),
            in_specs=[
                pl.BlockSpec((rows, columns), target(step))
                for step in range(line)
                for unused in range(count)
            ]
            + [fixed((EXTRA_ROWS, columns)) for unused in extras],
            out_specs=[fixed((cut_rows, columns))] * line,
        ),
        compiler_params=vmem_limit(60),
        name="cut_columns",
    )(place, group, *(list(weights) * line), *extras)


def order_shares(place, shares, count, vectors=0):
    line = len(shares)
    share_rows, columns = shares[0].shape
    rows = (share_rows - (EXTRA_ROWS if vectors else 0)) // count

    def kernel(place_ref, *refs):
        for step in range(line):
            source = lax.rem(place_ref[0] + line - step, line)
            for i in range(count):
                refs[line][source, i] = refs[step][i * rows : (i + 1) * rows]
            if vectors:
                lanes = pl.ds(pl.multiple_of(source * columns, columns), columns)
                refs[line + 1][:, lanes] = refs[step][count * rows :].astype(jnp.float32)

    shapes = [jax.ShapeDtypeStruct((line, count, rows, columns), shares[0].dtype)]
    if vectors:
        shapes.append(jax.ShapeDtypeStruct((EXTRA_ROWS, line * columns), jnp.float32))
    outs = pl.pallas_call(
        kernel,
        out_shape=shapes,
        in_specs=[whole(pltpu.SMEM)] + [whole()] * line,
        out_specs=[whole()] * len(shapes),
        compiler_params=vmem_limit(40),
        name="order_shares",
    )(place, *shares)
    return (outs[0], outs[1][:vectors]) if vectors else outs[0]


def widen_columns(place, shares, count, rows):
    line = len(shares)
    share_rows, columns = shares[0].shape

    def kernel(place_ref, *refs):
        for step in range(line):

            @pl.when(pl.program_id(0) == step)
            def widen(step=step):
                for i in range(count):
                    refs[line + i][...] = refs[step][i * rows : (i + 1) * rows].astype(jnp.float32)

    return pl.pallas_call(
        kernel,
        out_shape=[jax.ShapeDtypeStruct((rows, line * columns), jnp.float32)] * count,
        grid_spec=pltpu.PrefetchScalarGridSpec(
            num_scalar_prefetch=1,
            grid=(line,),
            in_specs=[pl.BlockSpec((share_rows, columns), lambda j, place: (0, 0))] * line,
            out_specs=[
                pl.BlockSpec(
                    (rows, columns), lambda j, place: (0, lax.rem(place[0] + line - j, line))
                )
            ]
            * count,
        ),
        compiler_params=vmem_limit(40),
        name="widen_columns",
    )(place, *shares)


def project(place, pieces, gain, w_heads, cosine, sine):
    line, count, part, width = w_heads.shape
    slots, share, model_width = pieces[0].shape
    rows = slots * share * line
    tile = width // 2
    heads = tile // HEAD_DIM
    n_pieces = len(pieces)
    half = HEAD_DIM // 2

    def kernel(place_ref, *refs):
        piece_refs = refs[:n_pieces]
        gain_ref, w_ref, cos_ref, sin_ref, rows_ref, out_ref = refs[n_pieces:]

        @pl.when((pl.program_id(0) == 0) & (pl.program_id(1) == 0))
        def assemble():
            spread(piece_refs, place_ref, rows_ref)
            rows_ref[...] = (rows_ref[...].astype(jnp.float32) * gain_ref[...]).astype(jnp.bfloat16)

        weight = w_ref[...].reshape(line * part, tile)
        turned = dot_f32(rows_ref[...], weight).T
        c, s = cos_ref[0], sin_ref[0]
        for head in range(heads):
            a = turned[head * HEAD_DIM : head * HEAD_DIM + half]
            b = turned[head * HEAD_DIM + half : (head + 1) * HEAD_DIM]
            out_ref[head, 0, :half, :] = (a * c - b * s).astype(jnp.bfloat16)
            out_ref[head, 0, half:, :] = (b * c + a * s).astype(jnp.bfloat16)

    return pl.pallas_call(
        kernel,
        grid=(count, 2),
        out_shape=[
            jax.ShapeDtypeStruct((rows, model_width), jnp.bfloat16),
            jax.ShapeDtypeStruct((width // HEAD_DIM, count, HEAD_DIM, rows), jnp.bfloat16),
        ],
        in_specs=[whole(pltpu.SMEM)]
        + [whole()] * (n_pieces + 1)
        + [
            pl.BlockSpec((line, 1, part, tile), lambda m, h: (0, m, 0, h)),
            pl.BlockSpec((1, half, rows), lambda m, h: (m, 0, 0)),
            pl.BlockSpec((1, half, rows), lambda m, h: (m, 0, 0)),
        ],
        out_specs=[
            pl.BlockSpec((rows, model_width), lambda m, h: (0, 0)),
            pl.BlockSpec((heads, 1, HEAD_DIM, rows), lambda m, h: (h, m, 0, 0)),
        ],
        compiler_params=vmem_limit(48),
        cost_estimate=work(6 * rows * model_width * width, 8 * rows * model_width),
        name="project",
    )(place, *pieces, gain, w_heads, cosine, sine)


def mix_out(place, mixed, w_out, slots, line):
    heads, unused, rows = mixed.shape
    width, model_width = w_out.shape
    share = rows // slots // line

    def kernel(place_ref, mixed_ref, w_ref, own_ref, *rest):
        *others, total = rest
        left = mixed_ref[...].reshape(width, rows).T
        total[...] = dot_f32(left, w_ref[...])
        deal(total, place_ref, own_ref, others)

    return pl.pallas_call(
        kernel,
        out_shape=dealt_shapes(slots, share, model_width, line),
        in_specs=[whole(pltpu.SMEM), whole(), whole()],
        out_specs=[whole()] * line,
        scratch_shapes=[pltpu.VMEM((rows, model_width), jnp.float32)],
        compiler_params=vmem_limit(48),
        cost_estimate=work(2 * rows * model_width * width, 8 * rows * model_width),
        name="mix_out",
    )(place, mixed, w_out)


def mlp_forward(place, pieces, upstream_pieces, w_mlp, tile):
    line, count, part, width = w_mlp.shape
    slots, share, model_width = pieces[0].shape
    rows = slots * share * line
    n_pieces = len(pieces)
    bf, f32 = jnp.bfloat16, jnp.float32

    def kernel(place_ref, *refs):
        x_pieces, u_pieces = refs[:n_pieces], refs[n_pieces : 2 * n_pieces]
        w_ref, x_ref, u_ref, hidden_ref, gate_ref, up_ref, own_ref = refs[
            2 * n_pieces : 2 * n_pieces + 7
        ]
        *others, total = refs[2 * n_pieces + 7 :]
        step = pl.program_id(0)

        @pl.when(step == 0)
        def assemble():
            spread(x_pieces, place_ref, x_ref)
            spread(u_pieces, place_ref, u_ref)

        down = w_ref[:, 0].reshape(line * part, tile)
        gate = w_ref[:, 1].reshape(line * part, tile)
        up = w_ref[:, 2].reshape(line * part, tile)
        x = x_ref[...]
        grad_hidden = dot_f32(u_ref[...], down)
        gate_act = dot_f32(x, gate)
        upward = dot_f32(x, up)
        sigmoid = jax.nn.sigmoid(gate_act)
        silu = gate_act * sigmoid
        hidden_ref[...] = (silu * upward).astype(bf)
        grad_gate = (
            grad_hidden * upward * sigmoid * (1.0 + gate_act * (1.0 - sigmoid))
        ).astype(bf)
        grad_up = (grad_hidden * silu).astype(bf)
        gate_ref[...] = grad_gate
        up_ref[...] = grad_up
        part_two = nt_dot(grad_gate, gate) + nt_dot(grad_up, up)

        @pl.when(step == 0)
        def first():
            total[...] = part_two

        @pl.when(step > 0)
        def further():
            total[...] += part_two

        @pl.when(step == pl.num_programs(0) - 1)
        def last():
            deal(total, place_ref, own_ref, others)

    fixed = lambda shape: pl.BlockSpec(shape, lambda j: (0,) * len(shape))
    columns = pl.BlockSpec((rows, tile), lambda j: (0, j))
    dealt = dealt_shapes(slots, share, model_width, line)
    return pl.pallas_call(
        kernel,
        grid=(width // tile,),
        out_shape=[jax.ShapeDtypeStruct((rows, model_width), bf)] * 2
        + [jax.ShapeDtypeStruct((rows, width), bf)] * 3
        + dealt,
        in_specs=[whole(pltpu.SMEM)]
        + [whole()] * (2 * n_pieces)
        + [pl.BlockSpec((line, count, part, tile), lambda j: (0, 0, 0, j))],
        out_specs=[fixed((rows, model_width))] * 2
        + [columns] * 3
        + [fixed((slots, share, model_width))] * line,
        scratch_shapes=[pltpu.VMEM((rows, model_width), f32)],
        compiler_params=vmem_limit(60),
        cost_estimate=work(16 * rows * model_width * width, 14 * model_width * width),
        name="mlp_forward",
    )(place, *pieces, *upstream_pieces, w_mlp)


def gate_up_weights(x_rows, grad_gate, grad_up, groups, line, tile):
    rows, model_width = x_rows.shape
    width = grad_gate.shape[1]
    block = model_width // groups // line

    def kernel(x_ref, gate_ref, up_ref, out_ref):
        for i, ref in enumerate((gate_ref, up_ref)):
            grads = transpose_product(x_ref[...], ref[...]).astype(jnp.bfloat16)
            out_ref[:, :, i * block : (i + 1) * block] = grads.reshape(groups, line, block, tile)

    columns = pl.BlockSpec((rows, tile), lambda j: (0, j))
    return pl.pallas_call(
        kernel,
        grid=(width // tile,),
        out_shape=jax.ShapeDtypeStruct((groups, line, 2 * block, width), jnp.bfloat16),
        in_specs=[pl.BlockSpec((rows, model_width), lambda j: (0, 0)), columns, columns],
        out_specs=pl.BlockSpec((groups, line, 2 * block, tile), lambda j: (0, 0, 0, j)),
        compiler_params=vmem_limit(60),
        cost_estimate=work(4 * rows * model_width * width, 8 * model_width * width),
        name="gate_up_weights",
    )(x_rows, grad_gate, grad_up)


def down_weights(u_rows, hidden, groups, line, tile):
    rows, model_width = u_rows.shape
    width = hidden.shape[1]
    block = model_width // groups // line

    def kernel(u_ref, hidden_ref, out_ref):
        grads = transpose_product(u_ref[...], hidden_ref[...]).astype(jnp.bfloat16)
        out_ref[:, :line] = grads.reshape(groups, line, block, tile)

    return pl.pallas_call(
        kernel,
        grid=(width // tile,),
        out_shape=jax.ShapeDtypeStruct((groups, line + 1, block, width), jnp.bfloat16),
        in_specs=[
            pl.BlockSpec((rows, model_width), lambda j: (0, 0)),
            pl.BlockSpec((rows, tile), lambda j: (0, j)),
        ],
        out_specs=pl.BlockSpec((groups, line + 1, block, tile), lambda j: (0, 0, 0, j)),
        compiler_params=vmem_limit(60),
        cost_estimate=work(2 * rows * model_width * width, 4 * model_width * width),
        name="down_weights",
    )(u_rows, hidden)


def mlp_out(place, hidden, w_mlp, slots, tile):
    line, count, part, width = w_mlp.shape
    rows = hidden.shape[0]
    model_width = line * part
    share = rows // slots // line

    def kernel(place_ref, hidden_ref, w_ref, own_ref, *rest):
        *others, total = rest
        step = pl.program_id(0)
        part_out = nt_dot(hidden_ref[...], w_ref[...].reshape(line * part, tile))

        @pl.when(step == 0)
        def first():
            total[...] = part_out

        @pl.when(step > 0)
        def further():
            total[...] += part_out

        @pl.when(step == pl.num_programs(0) - 1)
        def last():
            deal(total, place_ref, own_ref, others)

    fixed = lambda shape: pl.BlockSpec(shape, lambda j: (0,) * len(shape))
    return pl.pallas_call(
        kernel,
        grid=(width // tile,),
        out_shape=dealt_shapes(slots, share, model_width, line),
        in_specs=[
            whole(pltpu.SMEM),
            pl.BlockSpec((rows, tile), lambda j: (0, j)),
            pl.BlockSpec((line, 1, part, tile), lambda j: (0, 0, 0, j)),
        ],
        out_specs=[fixed((slots, share, model_width))] * line,
        scratch_shapes=[pltpu.VMEM((rows, model_width), jnp.float32)],
        compiler_params=vmem_limit(60),
        cost_estimate=work(2 * rows * model_width * width, 2 * model_width * width),
        name="mlp_out",
    )(place, hidden, w_mlp)


def branch_back(place, pieces, w_out, heads):
    slots, share, model_width = pieces[0].shape
    line = (len(pieces) + 1) // 2
    rows = slots * share * line

    def kernel(place_ref, *refs):
        *piece_refs, w_ref, rows_ref, out_ref = refs
        spread(piece_refs, place_ref, rows_ref)
        turned = nt_dot(w_ref[...], rows_ref[...])
        out_ref[...] = turned.astype(jnp.bfloat16).reshape(out_ref.shape)

    return pl.pallas_call(
        kernel,
        out_shape=[
            jax.ShapeDtypeStruct((rows, model_width), jnp.bfloat16),
            jax.ShapeDtypeStruct((heads, HEAD_DIM, rows), jnp.bfloat16),
        ],
        in_specs=[whole(pltpu.SMEM)] + [whole()] * (len(pieces) + 1),
        out_specs=[whole(), whole()],
        compiler_params=vmem_limit(40),
        cost_estimate=work(2 * rows * model_width * heads * HEAD_DIM, 8 * rows * model_width),
        name="branch_back",
    )(place, *pieces, w_out)


def out_weight(grads, mixed, branch_rows, tile):
    groups, blocks, block, width = grads.shape
    heads, unused, rows = mixed.shape

    def kernel(grads_ref, mixed_ref, rows_ref, out_ref):
        left = mixed_ref[...].reshape(heads * HEAD_DIM, rows)
        product = dot_f32(left, rows_ref[...]).astype(jnp.bfloat16)
        out_ref[...] = product.reshape(groups, 1, block, tile)

    return pl.pallas_call(
        kernel,
        grid=(width // tile,),
        out_shape=jax.ShapeDtypeStruct(grads.shape, grads.dtype),
        in_specs=[
            pl.BlockSpec(memory_space=pl.ANY),
            pl.BlockSpec(mixed.shape, lambda j: (0, 0, 0)),
            pl.BlockSpec((rows, tile), lambda j: (0, j)),
        ],
        out_specs=pl.BlockSpec((groups, 1, block, tile), lambda j: (0, blocks - 1, 0, j)),
        input_output_aliases={0: 0},
        compiler_params=vmem_limit(60),
        cost_estimate=work(4 * rows * heads * HEAD_DIM * width, 8 * rows * width),
        name="out_weight",
    )(grads, mixed, branch_rows)


def head_weights(group, all_rows, corner, head_grads, w_head, gain, gain_two, owners):
    sources, features, rows = head_grads.shape
    model_width = all_rows[0].shape[1]
    block = model_width // owners
    lanes = 2 * LANES
    half = rows // 2
    f32 = jnp.float32

    def kernel(group_ref, *refs):
        x_refs, corner_refs = refs[: sources - 2], refs[sources - 2 : sources + 2]
        g_ref, w_ref, gain_ref, two_ref, out_ref, total = refs[sources + 2 :]
        step = pl.program_id(0)

        def product(bits, ref):
            return dot_f32(g_ref[lax.bitwise_xor(group_ref[0], bits)], ref[...])

        part = sum(product(bits, ref) for bits, ref in enumerate(x_refs))

        def with_corner(half_refs):
            return part + product(sources - 2, half_refs[0]) + product(sources - 1, half_refs[1])

        @pl.when(step == 0)
        def first():
            total[...] = with_corner(corner_refs[0::2])

        @pl.when(step == 1)
        def last():
            grads = (total[...] + with_corner(corner_refs[1::2])).T
            weighed = jnp.sum(grads * w_ref[...].astype(f32), 1, keepdims=True) / gain_ref[...].T
            spare = lanes - features
            at = lax.broadcasted_iota(jnp.int32, (model_width, spare), 1)
            tail = jnp.where(at == 0, weighed, jnp.where(at == 1, two_ref[...].T, 0.0))
            joined = jnp.concatenate([grads, tail], 1).astype(jnp.bfloat16)
            out_ref[...] = joined.reshape(owners, block, lanes)

    fixed = lambda shape: pl.BlockSpec(shape, lambda s: (0,) * len(shape))
    return pl.pallas_call(
        kernel,
        grid=(2,),
        out_shape=jax.ShapeDtypeStruct((owners, block, lanes), jnp.bfloat16),
        in_specs=[whole(pltpu.SMEM)]
        + [pl.BlockSpec((half, model_width), lambda s: (s, 0))] * (sources - 2)
        + [fixed((half, model_width))] * 4
        + [
            pl.BlockSpec((sources, features, half), lambda s: (0, 0, s)),
            fixed((model_width, features)),
            fixed((1, model_width)),
            fixed((1, model_width)),
        ],
        out_specs=fixed((owners, block, lanes)),
        scratch_shapes=[pltpu.VMEM((features, model_width), f32)],
        compiler_params=vmem_limit(60),
        cost_estimate=work(6 * sources * rows * features * model_width, 0),
        name="head_weights",
    )(group, *all_rows, *corner, head_grads, w_head, gain, gain_two)


def join_heads(parts):
    groups, line, rows, lanes = parts.shape
    width = groups * HEAD_DIM

    def kernel(parts_ref, *outs):
        for i, out in enumerate(outs):
            pick = slice(i * HEAD_DIM, (i + 1) * HEAD_DIM)
            heads = [parts_ref[c, 0][:, pick].astype(jnp.float32) for c in range(groups)]
            out[...] = jnp.concatenate(heads, 1)

    return pl.pallas_call(
        kernel,
        grid=(line,),
        out_shape=[jax.ShapeDtypeStruct((rows, line * width), jnp.float32)] * 3,
        in_specs=[pl.BlockSpec((groups, 1, rows, lanes), lambda f: (0, f, 0, 0))],
        out_specs=[pl.BlockSpec((rows, width), lambda f: (0, f))] * 3,
        compiler_params=vmem_limit(24),
        name="join_heads",
    )(parts)


def project_back(place, head_grads, w_heads, slots):
    line, count, part, width = w_heads.shape
    rows, model_width = head_grads.shape[-1], line * part
    heads = width // HEAD_DIM
    share = rows // slots // line

    def kernel(place_ref, g_ref, w_ref, own_ref, *rest):
        *others, total = rest
        m = pl.program_id(0)
        grads = g_ref[...].reshape(width, rows).T
        partial = nt_dot(grads, w_ref[...].reshape(line * part, width))

        @pl.when(m == 0)
        def first():
            total[...] = partial

        @pl.when(m > 0)
        def further():
            total[...] += partial

        @pl.when(m == count - 1)
        def last():
            deal(total, place_ref, own_ref, others)

    fixed = lambda shape: pl.BlockSpec(shape, lambda m: (0,) * len(shape))
    return pl.pallas_call(
        kernel,
        grid=(count,),
        out_shape=dealt_shapes(slots, share, model_width, line),
        in_specs=[
            whole(pltpu.SMEM),
            pl.BlockSpec((heads, 1, HEAD_DIM, rows), lambda m: (0, m, 0, 0)),
            pl.BlockSpec((line, 1, part, width), lambda m: (0, m, 0, 0)),
        ],
        out_specs=[fixed((slots, share, model_width))] * line,
        scratch_shapes=[pltpu.VMEM((rows, model_width), jnp.float32)],
        compiler_params=vmem_limit(48),
        cost_estimate=work(2 * count * rows * width * model_width, 8 * rows * model_width),
        name="project_back",
    )(place, head_grads, w_heads)


def line_steps(size, step):
    return [(i, i + step) for i in range(size) if 0 <= i + step < size]


def after(values, *earlier):
    return lax.optimization_barrier((values, earlier))[0]


def send_shares(share, axis, between=()):
    size = lax.axis_size(axis)
    ups, downs = [share], [share]
    for hop in range(1, size):
        up = lax.ppermute(ups[-1], axis, line_steps(size, 1)[hop - 1 :])
        down = lax.ppermute(downs[-1], axis, line_steps(size, -1)[: size - hop])
        if hop <= len(between):
            done = between[hop - 1]((ups[-1], downs[-1]))
            up, down = after((up, down), done)
        ups.append(up)
        downs.append(down)
    return ups + downs[1:]


def flip(values, bits):
    size = lax.axis_size("ctx")
    return lax.ppermute(values, "ctx", [(i, i ^ bits) for i in range(size)])


def send_dealt(others, axis):
    size = lax.axis_size(axis)
    return [
        lax.ppermute(other, axis, [(i, (i + step) % size) for i in range(size)])
        for step, other in enumerate(others, 1)
    ]


def scatter_line(others, axis, between=()):
    size = lax.axis_size(axis)
    up = down = None
    for hop in range(1, size):
        rising, falling = others[size - hop - 1], others[hop - 1]
        if hop > 1:
            rising = (rising.astype(jnp.float32) + up.astype(jnp.float32)).astype(rising.dtype)
            falling = (falling.astype(jnp.float32) + down.astype(jnp.float32)).astype(falling.dtype)
        up = lax.ppermute(rising, axis, line_steps(size, 1)[:hop])
        down = lax.ppermute(falling, axis, line_steps(size, -1)[size - 1 - hop :])
        if hop <= len(between):
            up, down = after((up, down), between[hop - 1]((rising, falling)))
    return [up, down]


def add_shares(own, received):
    return own + sum(share.astype(jnp.float32) for share in received)


def swap_dealt(shares):
    return [shares[0]] + send_dealt(shares[1:], "fsdp")


def deal_line(parts, place):
    line = parts.shape[0]
    return [
        lax.dynamic_index_in_dim(parts, lax.rem(place[0] + step, line), 0, keepdims=False)
        for step in range(line)
    ]


def swap_heads(parts):
    return lax.all_to_all(parts, "ctx", split_axis=0, concat_axis=0, tiled=True)


def sum_groups(parts):
    return lax.psum_scatter(parts, "ctx", scatter_dimension=0, tiled=True)[0]


def head_device(
    tokens,
    block_order,
    w_query,
    w_key,
    w_value,
    w_out,
    w_gate,
    w_up,
    w_down,
    gain_attn,
    gain_mlp,
    cotangent,
):
    slots, share_rows, model_width = tokens.shape
    ctx_size, line = lax.axis_size("ctx"), lax.axis_size("fsdp")
    block_rows = share_rows * line
    group_rows = slots * block_rows
    bf, f32 = jnp.bfloat16, jnp.float32
    place = lax.axis_index("fsdp").astype(jnp.int32).reshape(1)
    group = lax.axis_index("ctx").astype(jnp.int32).reshape(1)
    own_rows = w_query.shape[0] // ctx_size
    order = block_order.astype(jnp.int32)
    long_tile = (8 if ctx_size * slots % 8 == 0 else 2) * block_rows
    slot_of = jnp.sum(
        jnp.where(order[None, :] == jnp.arange(order.shape[0])[:, None], jnp.arange(order.shape[0], dtype=jnp.int32)[None, :], 0), 1
    ).astype(jnp.int32)

    stream = tokens.astype(f32)
    root_one = lax.rsqrt(jnp.mean(stream * stream, -1, keepdims=True) + EPSILON)
    norm_one = stream * root_one
    gain_rows = jnp.pad(jnp.stack([gain_attn, gain_mlp]), ((0, EXTRA_ROWS - 2), (0, 0)))
    head_cuts = swap_dealt(
        cut_columns(place, group, [w_query, w_key, w_value], own_rows, line, gain_rows)
    )
    own_heads, gains = order_shares(place, head_cuts, 3, 2)
    attn_gain, mlp_gain = gains[0], gains[1]
    w_heads = lax.all_gather(own_heads, "ctx", axis=2, tiled=True)

    attn_pieces = send_shares(after(norm_one.astype(bf), head_cuts), "fsdp")

    mlp_cuts = cut_columns(place, group, [w_down, w_gate, w_up], own_rows, line)
    w_heads = after(w_heads, mlp_cuts)
    mlp_cuts = swap_dealt(after(mlp_cuts, attn_pieces))

    w_head = lax.dynamic_slice_in_dim(w_heads, group[0] * HEAD_DIM, HEAD_DIM, 3)
    w_head = jnp.concatenate([w_head[:, i].reshape(model_width, HEAD_DIM) for i in range(3)], 1)

    half = HEAD_DIM // 2
    frequency = 1.0 / ROPE_BASE ** (jnp.arange(half, dtype=f32) * (2.0 / HEAD_DIM))
    places = jnp.arange(group_rows * ctx_size, dtype=jnp.int32).astype(f32)
    angles = frequency[:, None] * places[None, :]
    cosine, sine = jnp.cos(angles), jnp.sin(angles)

    def own_columns(table):
        return jnp.concatenate(
            [
                lax.dynamic_slice_in_dim(
                    table, order[slots * group[0] + i] * block_rows, block_rows, 1
                )
                for i in range(slots)
            ],
            1,
        )

    own_cosine, own_sine = own_columns(cosine), own_columns(sine)
    turn_cosine = jnp.stack([own_cosine, own_cosine, jnp.ones_like(own_cosine)])
    turn_sine = jnp.stack([own_sine, own_sine, jnp.zeros_like(own_sine)])

    attn_rows, heads_out = project(
        place, attn_pieces, attn_gain[None], w_heads, turn_cosine, turn_sine
    )
    heads_out = heads_out.reshape(ctx_size, 3 * HEAD_DIM, group_rows)
    head_rows = swap_heads(after(heads_out, mlp_cuts[1]))
    mixed_send, attended, log_total = attend(
        order, head_rows, block_rows, long_tile, 2 * block_rows
    )
    mixed = swap_heads(mixed_send)
    mlp_cuts = order_shares(place, after(mlp_cuts, mixed), 3)
    w_mlp = lax.all_gather(mlp_cuts, "ctx", axis=2, tiled=True)
    upstream_pieces = send_shares(after(cotangent, mlp_cuts), "fsdp")
    own, *others = mix_out(place, after(mixed, w_head, mlp_cuts), w_out, slots, line)
    middle = stream + add_shares(own, scatter_line(others, "fsdp"))

    root_two = lax.rsqrt(jnp.mean(middle * middle, -1, keepdims=True) + EPSILON)
    norm_two = middle * root_two
    mlp_input = (norm_two * mlp_gain).astype(bf)
    mlp_pieces = send_shares(mlp_input, "fsdp")

    all_rows = {0: attn_rows}
    start_rows = after(attn_rows, mlp_pieces, upstream_pieces)
    all_rows[2], all_rows[4] = flip(start_rows, 2), flip(start_rows, 4)
    mlp_rows, upstream_rows, hidden, grad_gate, grad_up, own, *others = mlp_forward(
        place, mlp_pieces, upstream_pieces, w_mlp, 512
    )
    results = {}

    def weigh_gate_up(sent):
        rows_here = after(mlp_rows, sent)
        results["gate_up"] = gate_up_weights(rows_here, grad_gate, grad_up, ctx_size, line, 512)
        return results["gate_up"], all_rows[2], all_rows[4]

    upper = attn_rows.shape[0] // 2

    def weigh_down(sent):
        results["down"] = down_weights(
            upstream_rows, after(hidden, sent), ctx_size, line, 512
        )
        results["gate_up_sums"] = sum_groups(after(results["gate_up"], sent))
        return results["down"]

    grad_two = add_shares(own, scatter_line(others, "fsdp", (weigh_gate_up, weigh_down)))
    gate_up_sums = results["gate_up_sums"]
    down_grads = results["down"]
    gain_two_part = jnp.sum(grad_two * norm_two, (0, 1))
    grad_middle = cotangent.astype(f32) + norm_back(grad_two, norm_two, root_two, mlp_gain)

    def weigh_out(sent):
        results["out"] = mlp_out(place, after(hidden, sent), w_mlp, slots, 512)
        return results["out"]

    def cut_corner(sent):
        by_x, by_y = after((all_rows[2], all_rows[4]), sent)
        results["corner"] = (by_x[:upper], by_y[upper:])
        return results["corner"]

    branch_pieces = send_shares(grad_middle.astype(bf), "fsdp", (weigh_out, cut_corner))
    corner = [flip(results["corner"][0], 4), flip(results["corner"][1], 2)]
    own_out, *others_out = results["out"]
    branch_rows, grad_mixed = branch_back(place, branch_pieces, w_out, ctx_size)

    out_received = send_dealt(after(others_out, branch_rows), "fsdp")
    for bits in (0, 2, 4):
        all_rows[bits + 1] = flip(after(all_rows[bits], branch_rows), 1)
    grad_heads = swap_heads(grad_mixed)
    down_grads = out_weight(down_grads, mixed, branch_rows, 512)
    head_grads = attend_back(
        jnp.concatenate([order, slot_of]),
        head_rows,
        after(
            grad_heads, down_grads, all_rows[1], all_rows[3], all_rows[5]
        ),
        attended,
        log_total,
        cosine,
        sine,
        block_rows,
        long_tile,
        2 * block_rows,
    )
    head_grads = after(head_grads, out_received, corner)
    corner = corner + [flip(part, 1) for part in after(corner, head_grads)]
    gate_up_dealt = deal_line(after(gate_up_sums, head_grads), place)
    gate_up_back = swap_dealt(gate_up_dealt)
    down_sums = sum_groups(after(down_grads, gate_up_sums, head_grads))
    lin_grads = swap_heads(after(head_grads, gate_up_dealt))
    head_parts = head_weights(
        group,
        [all_rows[bits] for bits in range(ctx_size - 2)],
        corner,
        after(head_grads, gate_up_dealt),
        w_head,
        attn_gain[None],
        gain_two_part[None],
        ctx_size * line,
    )
    lin_grads = after(lin_grads, head_parts, gate_up_back[1], gate_up_back[2])
    head_parts = lax.all_to_all(
        after(head_parts, lin_grads), ("ctx", "fsdp"), split_axis=0, concat_axis=0, tiled=True
    )
    lin_grads = lin_grads.reshape(ctx_size, 3, HEAD_DIM, group_rows)
    own, *others = project_back(place, lin_grads, w_heads, slots)

    def swap_down(sent):
        parts = deal_line(after(down_sums, sent)[:line], place)
        results["down_back"] = swap_dealt(parts)
        return results["down_back"][1]

    one_received = scatter_line(
        others, "fsdp", (lambda sent: (gate_up_back[3], head_parts), lambda sent: (), swap_down)
    )
    down_back = results["down_back"]
    grad_one = add_shares(own, one_received)
    result = (middle + add_shares(own_out, out_received)).astype(bf)
    grad_tokens = grad_middle + norm_back(grad_one, norm_one, root_one, attn_gain)
    owners = [(c * line + f, f * ctx_size + c) for c in range(ctx_size) for f in range(line)]
    grad_w_out = lax.ppermute(down_sums[line], ("ctx", "fsdp"), owners).astype(f32)
    grad_w_gate, grad_w_up = widen_columns(place, gate_up_back, 2, own_rows)
    (grad_w_down,) = widen_columns(place, after(down_back, grad_tokens), 1, own_rows)
    head_parts = head_parts.reshape(ctx_size, line, own_rows, -1)
    grad_w_query, grad_w_key, grad_w_value = join_heads(head_parts)
    spare = 3 * HEAD_DIM
    gain_grads = jnp.sum(head_parts[..., spare : spare + 2].astype(f32), (0, 1)).T
    return (
        result,
        grad_tokens,
        grad_w_query,
        grad_w_key,
        grad_w_value,
        grad_w_out,
        grad_w_gate,
        grad_w_up,
        grad_w_down,
        gain_grads[0],
        gain_grads[1],
    )


def layer_step(*arrays):
    heads_here = arrays[0].shape[-1] // lax.axis_size("fsdp") // HEAD_DIM
    if heads_here == lax.axis_size("ctx") == 8:
        return head_device(*arrays)
    return per_device(*arrays)


def solution(mesh):
    in_specs = (
        P("ctx", "fsdp", None),
        P(),
        P("fsdp", None),
        P("fsdp", None),
        P("fsdp", None),
        P("fsdp", None),
        P("fsdp", None),
        P("fsdp", None),
        P("fsdp", None),
        P("fsdp"),
        P("fsdp"),
        P("ctx", "fsdp", None),
    )
    out_specs = (
        P("ctx", "fsdp", None),
        P("ctx", "fsdp", None),
        P(("ctx", "fsdp"), None),
        P(("ctx", "fsdp"), None),
        P(("ctx", "fsdp"), None),
        P(("ctx", "fsdp"), None),
        P(("ctx", "fsdp"), None),
        P(("ctx", "fsdp"), None),
        P(("ctx", "fsdp"), None),
        P(("ctx", "fsdp")),
        P(("ctx", "fsdp")),
    )
    return jax.shard_map(
        layer_step, mesh=mesh, in_specs=in_specs, out_specs=out_specs, check_vma=False
    )
```

profile of v0, /device:TPU:19, one launch (start us, length us, event | category | flops | bytes accessed | tf_op | source)
XLA Modules:
  0.0 667.2 jit_solution(13573996063038355411)
XLA Ops:
  17.8 9.0 %collective-permute-done.1.refs_2_ = bf16[208,512]{1,0:T(8,128)(2,1)S(1)} collective-permute-done((bf16[208,512]{1,0:T(8,128)(2,1)}, bf16[208,512]{1,0:T(8,128)(2,1)S(1)}, u32[]{:S(2)}, u32[]{:S(2)}) %collective-permute-start.1) | collective-permute-done | bytes 213024 | tf_op jit(solution)/shard_map/ppermute | solution.py:1297
  39.6 10.0 %collective-permute-done.3.refs_1_ = bf16[2,64,2048]{2,1,0:T(8,128)(2,1)S(1)} collective-permute-done((bf16[2,64,2048]{2,1,0:T(8,128)(2,1)S(1)}, bf16[2,64,2048]{2,1,0:T(8,128)(2,1)S(1)}, u32[]{:S(2)}, u32[]{:S(2)}) %collective-permute-start.3) | collective-permute-done | bytes 524320 | tf_op jit(solution)/shard_map/ppermute | solution.py:1279
  55.8 8.4 %collective-permute-done.4.refs_2_ = bf16[2,64,2048]{2,1,0:T(8,128)(2,1)S(1)} collective-permute-done((bf16[2,64,2048]{2,1,0:T(8,128)(2,1)S(1)}, bf16[2,64,2048]{2,1,0:T(8,128)(2,1)S(1)}, u32[]{:S(2)}, u32[]{:S(2)}) %collective-permute-start.4) | collective-permute-done | bytes 524320 | tf_op jit(solution)/shard_map/ppermute | solution.py:1279
  81.2 9.0 %project.1 = (bf16[512,2048]{1,0:T(8,128)(2,1)}, bf16[8,3,64,512]{3,2,1,0:T(8,128)(2,1)}) custom-call(s32[1]{0:T(128)} %bitcast.place_ref, bf16[2,64,2048]{2,1,0:T(8,128)(2,1)S(1)} %fusion.2.refs_0_, bf16[2,64,2048]{2,1,0:T(8,128)(2,1)S(1)} %collective-permute-done.3.refs_1_, bf16[2,64,2048]{2,1,0:T(8,128)(2,1)S(1)} %collective-permute-done.4.refs_2_, ...), custom_call_target="tpu_custom_call" | custom-call | flops 644245120 | bytes 1677721 | tf_op jit(solution)/shard_map/project/pallas_call | solution.py:889
  94.2 7.9 %all-to-all-start = ((bf16[8,192,512]{2,1,0:T(8,128)(2,1)}), bf16[8,192,512]{2,1,0:T(8,128)(2,1)S(1)}, u32[]{:S(2)}, u32[]{:S(2)}) async-start(bf16[8,192,512]{2,1,0:T(8,128)(2,1)} %bitcast.6), calls=%async_computation | async-start | bytes 3145728 | tf_op jit(solution)/shard_map/all_to_all | solution.py:1334
  107.3 14.4 %all-to-all-done.qkv_ref = bf16[8,192,512]{2,1,0:T(8,128)(2,1)S(1)} async-done(((bf16[8,192,512]{2,1,0:T(8,128)(2,1)}), bf16[8,192,512]{2,1,0:T(8,128)(2,1)S(1)}, u32[]{:S(2)}, u32[]{:S(2)}) %all-to-all-start) | async-done | bytes 1572896 | tf_op jit(solution)/shard_map/all_to_all | solution.py:1334
  121.6 18.2 %attend.1 = (bf16[8,64,512]{2,1,0:T(8,128)(2,1)}, f32[64,4096]{1,0:T(8,128)S(1)}, f32[1,4096]{1,0:T(1,128)S(1)}) custom-call(s32[16]{0:T(128)S(1)} %copy-done.29, bf16[8,192,512]{2,1,0:T(8,128)(2,1)S(1)} %all-to-all-done.qkv_ref), custom_call_target="tpu_custom_call" | custom-call | flops 4294967296 | bytes 2097152 | tf_op jit(solution)/shard_map/attend/pallas_call | solution.py:575
  145.8 10.8 %collective-permute-done.11.refs_3_ = bf16[192,2048]{1,0:T(8,128)(2,1)} collective-permute-done((bf16[192,2048]{1,0:T(8,128)(2,1)}, bf16[192,2048]{1,0:T(8,128)(2,1)}, u32[]{:S(2)}, u32[]{:S(2)}) %collective-permute-start.11) | collective-permute-done | bytes 786464 | tf_op jit(solution)/shard_map/ppermute | solution.py:1297
  169.2 13.6 %collective-permute-done.15 = bf16[2,64,2048]{2,1,0:T(8,128)(2,1)S(1)} collective-permute-done((bf16[2,64,2048]{2,1,0:T(8,128)(2,1)S(1)}, bf16[2,64,2048]{2,1,0:T(8,128)(2,1)S(1)}, u32[]{:S(2)}, u32[]{:S(2)}) %collective-permute-start.15) | collective-permute-done | bytes 524320 | tf_op jit(solution)/shard_map/ppermute | solution.py:1311
  188.6 8.9 %collective-permute-done.13 = bf16[2,64,2048]{2,1,0:T(8,128)(2,1)S(1)} collective-permute-done((bf16[2,64,2048]{2,1,0:T(8,128)(2,1)S(1)}, bf16[2,64,2048]{2,1,0:T(8,128)(2,1)S(1)}, u32[]{:S(2)}, u32[]{:S(2)}) %collective-permute-start.13) | collective-permute-done | bytes 524320 | tf_op jit(solution)/shard_map/ppermute | solution.py:1310
  247.8 8.3 %collective-permute-done.19.refs_2_ = bf16[2,64,2048]{2,1,0:T(8,128)(2,1)S(1)} collective-permute-done((bf16[2,64,2048]{2,1,0:T(8,128)(2,1)S(1)}, bf16[2,64,2048]{2,1,0:T(8,128)(2,1)S(1)}, u32[]{:S(2)}, u32[]{:S(2)}) %collective-permute-start.19) | collective-permute-done | bytes 524320 | tf_op jit(solution)/shard_map/ppermute | solution.py:1279
  265.3 11.2 %collective-permute-done.20.refs_3_ = bf16[2,64,2048]{2,1,0:T(8,128)(2,1)S(1)} collective-permute-done((bf16[2,64,2048]{2,1,0:T(8,128)(2,1)S(1)}, bf16[2,64,2048]{2,1,0:T(8,128)(2,1)S(1)}, u32[]{:S(2)}, u32[]{:S(2)}) %collective-permute-start.20) | collective-permute-done | bytes 524320 | tf_op jit(solution)/shard_map/ppermute | solution.py:1279
  278.7 15.0 %all-gather.5.cloned.1.call-done.refs_14_.w_ref = bf16[4,3,512,2048]{3,2,1,0:T(8,128)(2,1)} async-done(((bf16[4,3,64,2048]{3,2,1,0:T(8,128)(2,1)}), bf16[4,3,512,2048]{3,2,1,0:T(8,128)(2,1)}) %all-gather.5.cloned.1.call-update) | async-done | bytes 25165840 | tf_op jit(solution)/shard_map/all_gather | solution.py:1420
  293.7 33.4 %mlp_forward.1 = (bf16[512,2048]{1,0:T(8,128)(2,1)}, bf16[512,2048]{1,0:T(8,128)(2,1)}, bf16[512,2048]{1,0:T(8,128)(2,1)}, bf16[512,2048]{1,0:T(8,128)(2,1)}, bf...) custom-call(s32[1]{0:T(128)} %bitcast.place_ref, ...), custom_call_target="tpu_custom_call" | custom-call | flops 6871947776 | bytes 11744051 | tf_op jit(solution)/shard_map/mlp_forward/pallas_call | solution.py:989
  330.1 13.7 %gate_up_weights.1 = bf16[8,4,128,2048]{3,2,1,0:T(8,128)(2,1)} custom-call(bf16[512,2048]{1,0:T(8,128)(2,1)} %get-tuple-element.143.x_ref, bf16[512,2048]{1,0:T(8,128)(2,1)} %get-tuple-element.144.gate_ref, bf16[512,2048]{1,0:T(8,128)(2,1)} %get-tuple-element.145.up_ref), custom_call_target="tpu_custom_call" | custom-call | flops 1717986944 | bytes 6710886 | tf_op jit(solution)/shard_map/gate_up_weights/pallas_call | solution.py:1019
  352.1 9.0 %down_weights.1.grads_ref = bf16[8,5,64,2048]{3,2,1,0:T(8,128)(2,1)} custom-call(bf16[512,2048]{1,0:T(8,128)(2,1)} %get-tuple-element.150.u_ref, bf16[512,2048]{1,0:T(8,128)(2,1)} %get-tuple-element.154.hidden_ref), custom_call_target="tpu_custom_call" | custom-call | flops 858993472 | bytes 3355443 | tf_op jit(solution)/shard_map/down_weights/pallas_call | solution.py:1040
  372.1 7.5 %collective-permute-done.36 = bf16[2,64,2048]{2,1,0:T(8,128)(2,1)S(1)} collective-permute-done((bf16[2,64,2048]{2,1,0:T(8,128)(2,1)S(1)}, bf16[2,64,2048]{2,1,0:T(8,128)(2,1)S(1)}, u32[]{:S(2)}, u32[]{:S(2)}) %collective-permute-start.36) | collective-permute-done | bytes 524320 | tf_op jit(solution)/shard_map/ppermute | solution.py:1310
  390.1 10.6 %mlp_out.1 = (f32[2,64,2048]{2,1,0:T(8,128)}, bf16[2,64,2048]{2,1,0:T(8,128)(2,1)}, bf16[2,64,2048]{2,1,0:T(8,128)(2,1)}, bf16[2,64,2048]{2,1,0:T(8,128)(2,1)}) custom-call(s32[1]{0:T(128)} %bitcast.place_ref, bf16[512,2048]{1,0:T(8,128)(2,1)} %get-tuple-element.154.hidden_ref, bf16[4,3,512,2048]{3,2,1,0:T(8,128)(2,1)} %all-gather.5.cloned.1.call-done.refs_14_.w_ref), custom_call_target="tpu_custom_call" | custom-call | flops 858993472 | bytes 1677721 | tf_op jit(solution)/shard_map/mlp_out/pallas_call | solution.py:1079
  451.4 30.4 %attend_back.1.refs_10_ = bf16[8,192,512]{2,1,0:T(8,128)(2,1)} custom-call(s32[32]{0:T(128)S(1)} %pad_add_fusion.order_ref, bf16[8,192,512]{2,1,0:T(8,128)(2,1)S(1)} %copy-done.6, bf16[8,64,512]{2,1,0:T(8,128)(2,1)S(1)} %all-to-all-done.2.go_ref, f32[64,4096]{1,0:T(8,128)S(1)} %copy-done.31, f32[1,4096]{1,0:T(1,128)S(1)} %get-tuple-element.175.lse_ref, ...), custom_call_target="tpu_custom_call" | custom-call | flops 6871947776 | bytes 4194304 | tf_op jit(solution)/shard_map/attend_back/pallas_call | solution.py:688
  509.3 13.3 %head_weights.1 = bf16[32,64,256]{2,1,0:T(8,128)(2,1)} custom-call(s32[1]{0:T(128)} %bitcast.1.group_ref, bf16[512,2048]{1,0:T(8,128)(2,1)} %get-tuple-element.170.refs_0_, bf16[512,2048]{1,0:T(8,128)(2,1)} %collective-permute-done.47.refs_1_, bf16[512,2048]{1,0:T(8,128)(2,1)} %collective-permute-done.32.refs_2_, ...), custom_call_target="tpu_custom_call" | custom-call | flops 1932735232 | tf_op jit(solution)/shard_map/head_weights/pallas_call | solution.py:1183
  523.4 12.7 %collective-permute-done.55.refs_2_ = bf16[128,2048]{1,0:T(8,128)(2,1)S(1)} collective-permute-done((bf16[128,2048]{1,0:T(8,128)(2,1)S(1)}, bf16[128,2048]{1,0:T(8,128)(2,1)S(1)}, u32[]{:S(2)}, u32[]{:S(2)}) %collective-permute-start.55) | collective-permute-done | bytes 524320 | tf_op jit(solution)/shard_map/ppermute | solution.py:1297
  536.9 9.4 %all-to-all-start.4 = ((bf16[32,64,256]{2,1,0:T(8,128)(2,1)}), bf16[32,64,256]{2,1,0:T(8,128)(2,1)S(1)}, u32[]{:S(2)}, u32[]{:S(2)}) async-start(bf16[32,64,256]{2,1,0:T(8,128)(2,1)} %head_weights.1), calls=%async_computation.5 | async-start | bytes 2097152 | tf_op jit(solution)/shard_map/all_to_all | solution.py:1508
  557.4 22.8 %collective-permute-done.58.refs_3_ = bf16[128,2048]{1,0:T(8,128)(2,1)S(1)} collective-permute-done((bf16[128,2048]{1,0:T(8,128)(2,1)}, bf16[128,2048]{1,0:T(8,128)(2,1)S(1)}, u32[]{:S(2)}, u32[]{:S(2)}) %collective-permute-start.58) | collective-permute-done | bytes 524320 | tf_op jit(solution)/shard_map/ppermute | solution.py:1297
  642.6 16.9 %collective-permute-done.64 = bf16[64,2048]{1,0:T(8,128)(2,1)S(1)} collective-permute-done((bf16[64,2048]{1,0:T(8,128)(2,1)S(1)}, bf16[64,2048]{1,0:T(8,128)(2,1)S(1)}, u32[]{:S(2)}, u32[]{:S(2)}) %collective-permute-start.64) | collective-permute-done | bytes 262176 | tf_op jit(solution)/shard_map/ppermute | solution.py:1527
  (320 shorter events, 326.2 us)
Async XLA Ops:
  7.2 74.0 %all-gather.3.cloned.1.call-start = ((), (), s32[]{:S(2)}) async-start(), calls=%async_computation.7 | async-start | bytes 7077888 | tf_op jit(solution)/shard_map/all_gather | solution.py:1378
  94.2 27.5 %all-to-all-start = ((bf16[8,192,512]{2,1,0:T(8,128)(2,1)}), bf16[8,192,512]{2,1,0:T(8,128)(2,1)S(1)}, u32[]{:S(2)}, u32[]{:S(2)}) async-start(bf16[8,192,512]{2,1,0:T(8,128)(2,1)} %bitcast.6), calls=%async_computation | async-start | bytes 3145728 | tf_op jit(solution)/shard_map/all_to_all | solution.py:1334
  102.1 43.7 %collective-permute-start.10 = (bf16[192,2048]{1,0:T(8,128)(2,1)}, bf16[192,2048]{1,0:T(8,128)(2,1)}, u32[]{:S(2)}, u32[]{:S(2)}) collective-permute-start(bf16[192,2048]{1,0:T(8,128)(2,1)} %get-tuple-element.125), channel_id=1, source_target_pairs={{0,2},{1,3},{2,0},{3,1},{4,6},{5,7},{6,4},{7,5},{8,10},{9,11},{10,... | collective-permute-start | bytes 2359304 | tf_op jit(solution)/shard_map/ppermute | solution.py:1297
  107.3 49.3 %collective-permute-start.11 = (bf16[192,2048]{1,0:T(8,128)(2,1)}, bf16[192,2048]{1,0:T(8,128)(2,1)}, u32[]{:S(2)}, u32[]{:S(2)}) collective-permute-start(bf16[192,2048]{1,0:T(8,128)(2,1)} %get-tuple-element.126), channel_id=1, source_target_pairs={{0,3},{1,0},{2,1},{3,2},{4,7},{5,4},{6,5},{7,6},{8,11},{9,8},{10,9... | collective-permute-start | bytes 2359304 | tf_op jit(solution)/shard_map/ppermute | solution.py:1297
  145.8 147.9 %all-gather.5.cloned.1.call-start = ((), (), s32[]{:S(2)}) async-start(), calls=%async_computation.8 | async-start | bytes 28311552 | tf_op jit(solution)/shard_map/all_gather | solution.py:1420
  161.3 331.3 %reduce-scatter.3.cloned.1.call-start = ((), (), s32[]{:S(2)}) async-start(), calls=%async_computation.9 | async-start | bytes 18874368 | tf_op jit(solution)/shard_map/reduce_scatter | solution.py:1338
  224.6 22.5 %collective-permute-start.28 = (bf16[2,64,2048]{2,1,0:T(8,128)(2,1)S(1)}, bf16[2,64,2048]{2,1,0:T(8,128)(2,1)S(1)}, u32[]{:S(2)}, u32[]{:S(2)}) collective-permute-start(bf16[2,64,2048]{2,1,0:T(8,128)(2,1)S(1)} %collective-permute-done.27.refs_11_), channel_id=1, source_target_pairs={{1,0},{2,1},{5,4},{6,5},{9,8},{10,9},{13,12},{14,13},{17,16},{18,1... | collective-permute-start | bytes 1572872 | tf_op jit(solution)/shard_map/ppermute | solution.py:1280
  235.8 22.5 %collective-permute-start.22 = (bf16[2,64,2048]{2,1,0:T(8,128)(2,1)S(1)}, bf16[2,64,2048]{2,1,0:T(8,128)(2,1)S(1)}, u32[]{:S(2)}, u32[]{:S(2)}) collective-permute-start(bf16[2,64,2048]{2,1,0:T(8,128)(2,1)S(1)} %collective-permute-done.21.refs_4_), channel_id=1, source_target_pairs={{1,0},{2,1},{5,4},{6,5},{9,8},{10,9},{13,12},{14,13},{17,16},{18,1... | collective-permute-start | bytes 1572872 | tf_op jit(solution)/shard_map/ppermute | solution.py:1280
  276.6 67.2 %collective-permute-start.32 = (bf16[512,2048]{1,0:T(8,128)(2,1)}, bf16[512,2048]{1,0:T(8,128)(2,1)}, u32[]{:S(2)}, u32[]{:S(2)}) collective-permute-start(bf16[512,2048]{1,0:T(8,128)(2,1)} %get-tuple-element.170.refs_0_), channel_id=1, source_target_pairs={{0,8},{4,12},{8,0},{12,4},{16,24},{20,28},{24,16},{28,20},{1,9},{5... | collective-permute-start | bytes 6291464 | tf_op jit(solution)/shard_map/ppermute | solution.py:1291
  277.5 66.2 %collective-permute-start.33 = (bf16[512,2048]{1,0:T(8,128)(2,1)}, bf16[512,2048]{1,0:T(8,128)(2,1)}, u32[]{:S(2)}, u32[]{:S(2)}) collective-permute-start(bf16[512,2048]{1,0:T(8,128)(2,1)} %get-tuple-element.170.refs_0_), channel_id=1, source_target_pairs={{0,16},{4,20},{8,24},{12,28},{16,0},{20,4},{24,8},{28,12},{1,17},{... | collective-permute-start | bytes 6291464 | tf_op jit(solution)/shard_map/ppermute | solution.py:1291
  435.3 175.9 %reduce-scatter.5.cloned.1.call-start = ((), (), s32[]{:S(2)}) async-start(), calls=%async_computation.10 | async-start | bytes 11796480 | tf_op jit(solution)/shard_map/reduce_scatter | solution.py:1338
  435.3 53.3 %collective-permute-start.50 = (bf16[256,2048]{1,0:T(8,128)(2,1)}, bf16[256,2048]{1,0:T(8,128)(2,1)}, u32[]{:S(2)}, u32[]{:S(2)}) collective-permute-start(bf16[256,2048]{1,0:T(8,128)(2,1)} %slice.45), channel_id=1, source_target_pairs={{0,16},{4,20},{8,24},{12,28},{16,0},{20,4},{24,8},{28,12},{1,17},{... | collective-permute-start | bytes 3145736 | tf_op jit(solution)/shard_map/ppermute | solution.py:1291
  436.5 52.1 %collective-permute-start.51 = (bf16[256,2048]{1,0:T(8,128)(2,1)}, bf16[256,2048]{1,0:T(8,128)(2,1)}, u32[]{:S(2)}, u32[]{:S(2)}) collective-permute-start(bf16[256,2048]{1,0:T(8,128)(2,1)} %slice.46), channel_id=1, source_target_pairs={{0,8},{4,12},{8,0},{12,4},{16,24},{20,28},{24,16},{28,20},{1,9},{5... | collective-permute-start | bytes 3145736 | tf_op jit(solution)/shard_map/ppermute | solution.py:1291
  442.0 46.6 %collective-permute-start.44 = (bf16[2,64,2048]{2,1,0:T(8,128)(2,1)}, bf16[2,64,2048]{2,1,0:T(8,128)(2,1)}, u32[]{:S(2)}, u32[]{:S(2)}) collective-permute-start(bf16[2,64,2048]{2,1,0:T(8,128)(2,1)} %get-tuple-element.166), channel_id=1, source_target_pairs={{0,1},{1,2},{2,3},{3,0},{4,5},{5,6},{6,7},{7,4},{8,9},{9,10},{10,1... | collective-permute-start | bytes 1572872 | tf_op jit(solution)/shard_map/ppermute | solution.py:1297
  444.5 44.1 %collective-permute-start.45 = (bf16[2,64,2048]{2,1,0:T(8,128)(2,1)}, bf16[2,64,2048]{2,1,0:T(8,128)(2,1)}, u32[]{:S(2)}, u32[]{:S(2)}) collective-permute-start(bf16[2,64,2048]{2,1,0:T(8,128)(2,1)} %get-tuple-element.167), channel_id=1, source_target_pairs={{0,2},{1,3},{2,0},{3,1},{4,6},{5,7},{6,4},{7,5},{8,10},{9,11},{10,... | collective-permute-start | bytes 1572872 | tf_op jit(solution)/shard_map/ppermute | solution.py:1297
  447.7 44.8 %collective-permute-start.46 = (bf16[2,64,2048]{2,1,0:T(8,128)(2,1)}, bf16[2,64,2048]{2,1,0:T(8,128)(2,1)}, u32[]{:S(2)}, u32[]{:S(2)}) collective-permute-start(bf16[2,64,2048]{2,1,0:T(8,128)(2,1)} %get-tuple-element.168), channel_id=1, source_target_pairs={{0,3},{1,0},{2,1},{3,2},{4,7},{5,4},{6,5},{7,6},{8,11},{9,8},{10,9... | collective-permute-start | bytes 1572872 | tf_op jit(solution)/shard_map/ppermute | solution.py:1297
  495.3 41.6 %all-to-all-start.3 = ((bf16[8,192,512]{2,1,0:T(8,128)(2,1)}), bf16[8,192,512]{2,1,0:T(8,128)(2,1)S(1)}, u32[]{:S(2)}, u32[]{:S(2)}) async-start(bf16[8,192,512]{2,1,0:T(8,128)(2,1)} %attend_back.1.refs_10_), calls=%async_computation.4 | async-start | bytes 3145728 | tf_op jit(solution)/shard_map/all_to_all | solution.py:1334
  502.4 33.7 %collective-permute-start.55 = (bf16[128,2048]{1,0:T(8,128)(2,1)S(1)}, bf16[128,2048]{1,0:T(8,128)(2,1)S(1)}, u32[]{:S(2)}, u32[]{:S(2)}) collective-permute-start(bf16[128,2048]{1,0:T(8,128)(2,1)S(1)} %copy-done.59), channel_id=1, source_target_pairs={{0,2},{1,3},{2,0},{3,1},{4,6},{5,7},{6,4},{7,5},{8,10},{9,11},{10,... | collective-permute-start | bytes 1572872 | tf_op jit(solution)/shard_map/ppermute | solution.py:1297
  536.9 50.9 %all-to-all-start.4 = ((bf16[32,64,256]{2,1,0:T(8,128)(2,1)}), bf16[32,64,256]{2,1,0:T(8,128)(2,1)S(1)}, u32[]{:S(2)}, u32[]{:S(2)}) async-start(bf16[32,64,256]{2,1,0:T(8,128)(2,1)} %head_weights.1), calls=%async_computation.5 | async-start | bytes 2097152 | tf_op jit(solution)/shard_map/all_to_all | solution.py:1508
  546.2 33.9 %collective-permute-start.58 = (bf16[128,2048]{1,0:T(8,128)(2,1)}, bf16[128,2048]{1,0:T(8,128)(2,1)S(1)}, u32[]{:S(2)}, u32[]{:S(2)}) collective-permute-start(bf16[128,2048]{1,0:T(8,128)(2,1)} %get-tuple-element.215), channel_id=1, source_target_pairs={{0,3},{1,0},{2,1},{3,2},{4,7},{5,4},{6,5},{7,6},{8,11},{9,8},{10,9... | collective-permute-start | bytes 1572872 | tf_op jit(solution)/shard_map/ppermute | solution.py:1297
  555.2 25.7 %collective-permute-start.56 = (bf16[2,64,2048]{2,1,0:T(8,128)(2,1)S(1)}, bf16[2,64,2048]{2,1,0:T(8,128)(2,1)S(1)}, u32[]{:S(2)}, u32[]{:S(2)}) collective-permute-start(bf16[2,64,2048]{2,1,0:T(8,128)(2,1)S(1)} %get-tuple-element.186), channel_id=1, source_target_pairs={{0,1},{4,5},{8,9},{12,13},{16,17},{20,21},{24,25},{28,29}} | collective-permute-start | bytes 1572872 | tf_op jit(solution)/shard_map/ppermute | solution.py:1310
  556.1 31.7 %collective-permute-start.57 = (bf16[2,64,2048]{2,1,0:T(8,128)(2,1)S(1)}, bf16[2,64,2048]{2,1,0:T(8,128)(2,1)}, u32[]{:S(2)}, u32[]{:S(2)}) collective-permute-start(bf16[2,64,2048]{2,1,0:T(8,128)(2,1)S(1)} %get-tuple-element.184), channel_id=1, source_target_pairs={{3,2},{7,6},{11,10},{15,14},{19,18},{23,22},{27,26},{31,30}} | collective-permute-start | bytes 1572872 | tf_op jit(solution)/shard_map/ppermute | solution.py:1311
  615.5 25.2 %collective-permute-start.66 = (bf16[64,2048]{1,0:T(8,128)(2,1)S(1)}, bf16[64,2048]{1,0:T(8,128)(2,1)S(1)}, u32[]{:S(2)}, u32[]{:S(2)}) collective-permute-start(bf16[64,2048]{1,0:T(8,128)(2,1)S(1)} %get-tuple-element.219), channel_id=1, source_target_pairs={{0,3},{1,0},{2,1},{3,2},{4,7},{5,4},{6,5},{7,6},{8,11},{9,8},{10,9... | collective-permute-start | bytes 786440 | tf_op jit(solution)/shard_map/ppermute | solution.py:1297
  619.0 40.5 %collective-permute-start.64 = (bf16[64,2048]{1,0:T(8,128)(2,1)S(1)}, bf16[64,2048]{1,0:T(8,128)(2,1)S(1)}, u32[]{:S(2)}, u32[]{:S(2)}) collective-permute-start(bf16[64,2048]{1,0:T(8,128)(2,1)S(1)} %slice_bitcast_fusion), channel_id=1, source_target_pairs={{0,0},{1,8},{2,16},{3,24},{4,1},{5,9},{6,17},{7,25},{8,2},{9,10},{... | collective-permute-start | bytes 786440 | tf_op jit(solution)/shard_map/ppermute | solution.py:1527
  (112 other events, 1715.0 us)
Sparse Core Ops, SparseCore 0:
  33.4 47.7 all-gather.2
  161.4 132.2 all-gather.4
  346.9 141.2 reduce-scatter.2
  492.7 94.3 reduce-scatter.4
where the time goes:
time: 678 us; the launch traced here: 667 us
  waiting for transfers between devices  267 us (39%)
  Pallas kernels  169 us (25%)
  starting transfers between devices  168 us (25%)
  local copies, waits for them, and re-layouts  27.1 us (4%)
  other arithmetic  19.7 us (3%)
  between operations  16.6 us (2%)
    ppermute x15, waiting for transfers between devices, send_dealt(): lax.ppermute(other, axis, [(i, (i + step) % size) for i in range(size)])  81.4 us
    ppermute x12, waiting for transfers between devices, send_shares(): up = lax.ppermute(ups[-1], axis, line_steps(size, 1)[hop - 1:])  68.9 us
    pallas_call x1, Pallas kernels, mlp_forward(): pl.pallas_call(kernel, grid=(width // tile,), out_shape=[jax.ShapeDtypeSt...  33.4 us
    ppermute x9, waiting for transfers between devices, scatter_line(): down = lax.ppermute(falling, axis, line_steps(size, -1)[size - 1 - hop:])  31.7 us
    pallas_call x1, Pallas kernels, attend_back(): pl.pallas_call(functools.partial(bwd_kernel, block=block, tile=tile, step...  30.4 us
    ppermute x12, starting transfers between devices, send_shares(): down = lax.ppermute(downs[-1], axis, line_steps(size, -1)[:size - hop])  30.4 us
    ppermute x9, starting transfers between devices, scatter_line(): down = lax.ppermute(falling, axis, line_steps(size, -1)[size - 1 - hop:])  26.6 us
    ppermute x12, starting transfers between devices, send_shares(): up = lax.ppermute(ups[-1], axis, line_steps(size, 1)[hop - 1:])  25.1 us
  transfers between devices with their start and end apart: 76, of which 42 were waited for; matrix products, arithmetic and copies ran while one was open for 4% of the time, Pallas kernels for 24%

commit v1 on v0

--- a/solution.py
+++ b/solution.py
@@ -1361,7 +1361,7 @@
     group = lax.axis_index("ctx").astype(jnp.int32).reshape(1)
     own_rows = w_query.shape[0] // ctx_size
     order = block_order.astype(jnp.int32)
-    long_tile = (8 if ctx_size * slots % 8 == 0 else 2) * block_rows
+    sequence = group_rows * ctx_size
     slot_of = jnp.sum(
         jnp.where(order[None, :] == jnp.arange(order.shape[0])[:, None], jnp.arange(order.shape[0], dtype=jnp.int32)[None, :], 0), 1
     ).astype(jnp.int32)
@@ -1413,7 +1413,7 @@
     heads_out = heads_out.reshape(ctx_size, 3 * HEAD_DIM, group_rows)
     head_rows = swap_heads(after(heads_out, mlp_cuts[1]))
     mixed_send, attended, log_total = attend(
-        order, head_rows, block_rows, long_tile, 2 * block_rows
+        order, head_rows, block_rows, sequence, 2 * block_rows
     )
     mixed = swap_heads(mixed_send)
     mlp_cuts = order_shares(place, after(mlp_cuts, mixed), 3)
@@ -1428,7 +1428,7 @@
     mlp_pieces = send_shares(mlp_input, "fsdp")
 
     all_rows = {0: attn_rows}
-    start_rows = after(attn_rows, mlp_pieces, upstream_pieces)
+    start_rows = after(attn_rows, mlp_pieces, upstream_pieces, w_mlp)
     all_rows[2], all_rows[4] = flip(start_rows, 2), flip(start_rows, 4)
     mlp_rows, upstream_rows, hidden, grad_gate, grad_up, own, *others = mlp_forward(
         place, mlp_pieces, upstream_pieces, w_mlp, 512
@@ -1485,8 +1485,8 @@
         cosine,
         sine,
         block_rows,
-        long_tile,
-        2 * block_rows,
+        sequence,
+        block_rows,
     )
     head_grads = after(head_grads, out_received, corner)
     corner = corner + [flip(part, 1) for part in after(corner, head_grads)]

time: 678 us -> 669 us (0.987)
    unnamed x120 -> x118, local copies, waits for them, and re-layouts: 13.9 us -> 14 us
  transfers between devices with their start and end apart: 76 -> 76, of which waited for: 42 -> 40; matrix products, arithmetic and copies ran while one was open for 4% -> 4% of each run, Pallas kernels for 24% -> 24%
where the time goes in v1:
time: 669 us; the launch traced here: 662 us
  waiting for transfers between devices  266 us (40%)
  starting transfers between devices  168 us (25%)
  Pallas kernels  166 us (25%)
  local copies, waits for them, and re-layouts  27.2 us (4%)
  other arithmetic  19.6 us (3%)
  between operations  16.3 us (2%)
    ppermute x15, waiting for transfers between devices, send_dealt(): lax.ppermute(other, axis, [(i, (i + step) % size) for i in range(size)])  83.4 us
    ppermute x12, waiting for transfers between devices, send_shares(): up = lax.ppermute(ups[-1], axis, line_steps(size, 1)[hop - 1:])  66.6 us
    pallas_call x1, Pallas kernels, mlp_forward(): pl.pallas_call(kernel, grid=(width // tile,), out_shape=[jax.ShapeDtypeSt...  33.8 us
    ppermute x9, waiting for transfers between devices, scatter_line(): down = lax.ppermute(falling, axis, line_steps(size, -1)[size - 1 - hop:])  31.3 us
    ppermute x12, starting transfers between devices, send_shares(): down = lax.ppermute(downs[-1], axis, line_steps(size, -1)[:size - hop])  31.1 us
    pallas_call x1, Pallas kernels, attend_back(): pl.pallas_call(functools.partial(bwd_kernel, block=block, tile=tile, step...  27.8 us
    ppermute x9, starting transfers between devices, scatter_line(): down = lax.ppermute(falling, axis, line_steps(size, -1)[size - 1 - hop:])  26.5 us
    ppermute x12, starting transfers between devices, send_shares(): up = lax.ppermute(ups[-1], axis, line_steps(size, 1)[hop - 1:])  25.2 us
  transfers between devices with their start and end apart: 76, of which 40 were waited for; matrix products, arithmetic and copies ran while one was open for 4% of the time, Pallas kernels for 24%

profile of v1, /device:TPU:19, one launch (start us, length us, event | category | flops | bytes accessed | tf_op | source)
XLA Modules:
  0.0 661.8 jit_solution(11680891718943190899)
XLA Ops:
  17.8 9.0 %collective-permute-done.1.refs_2_ = bf16[208,512]{1,0:T(8,128)(2,1)S(1)} collective-permute-done((bf16[208,512]{1,0:T(8,128)(2,1)}, bf16[208,512]{1,0:T(8,128)(2,1)S(1)}, u32[]{:S(2)}, u32[]{:S(2)}) %collective-permute-start.1) | collective-permute-done | bytes 213024 | tf_op jit(solution)/shard_map/ppermute | solution.py:1297
  39.6 10.0 %collective-permute-done.3.refs_1_ = bf16[2,64,2048]{2,1,0:T(8,128)(2,1)S(1)} collective-permute-done((bf16[2,64,2048]{2,1,0:T(8,128)(2,1)S(1)}, bf16[2,64,2048]{2,1,0:T(8,128)(2,1)S(1)}, u32[]{:S(2)}, u32[]{:S(2)}) %collective-permute-start.3) | collective-permute-done | bytes 524320 | tf_op jit(solution)/shard_map/ppermute | solution.py:1279
  55.8 8.4 %collective-permute-done.4.refs_2_ = bf16[2,64,2048]{2,1,0:T(8,128)(2,1)S(1)} collective-permute-done((bf16[2,64,2048]{2,1,0:T(8,128)(2,1)S(1)}, bf16[2,64,2048]{2,1,0:T(8,128)(2,1)S(1)}, u32[]{:S(2)}, u32[]{:S(2)}) %collective-permute-start.4) | collective-permute-done | bytes 524320 | tf_op jit(solution)/shard_map/ppermute | solution.py:1279
  81.2 9.0 %project.1 = (bf16[512,2048]{1,0:T(8,128)(2,1)}, bf16[8,3,64,512]{3,2,1,0:T(8,128)(2,1)}) custom-call(s32[1]{0:T(128)} %bitcast.place_ref, bf16[2,64,2048]{2,1,0:T(8,128)(2,1)S(1)} %fusion.2.refs_0_, bf16[2,64,2048]{2,1,0:T(8,128)(2,1)S(1)} %collective-permute-done.3.refs_1_, bf16[2,64,2048]{2,1,0:T(8,128)(2,1)S(1)} %collective-permute-done.4.refs_2_, ...), custom_call_target="tpu_custom_call" | custom-call | flops 644245120 | bytes 1677721 | tf_op jit(solution)/shard_map/project/pallas_call | solution.py:889
  94.2 7.9 %all-to-all-start = ((bf16[8,192,512]{2,1,0:T(8,128)(2,1)}), bf16[8,192,512]{2,1,0:T(8,128)(2,1)S(1)}, u32[]{:S(2)}, u32[]{:S(2)}) async-start(bf16[8,192,512]{2,1,0:T(8,128)(2,1)} %bitcast.6), calls=%async_computation | async-start | bytes 3145728 | tf_op jit(solution)/shard_map/all_to_all | solution.py:1334
  107.3 14.4 %all-to-all-done.qkv_ref = bf16[8,192,512]{2,1,0:T(8,128)(2,1)S(1)} async-done(((bf16[8,192,512]{2,1,0:T(8,128)(2,1)}), bf16[8,192,512]{2,1,0:T(8,128)(2,1)S(1)}, u32[]{:S(2)}, u32[]{:S(2)}) %all-to-all-start) | async-done | bytes 1572896 | tf_op jit(solution)/shard_map/all_to_all | solution.py:1334
  121.6 16.9 %attend.1 = (bf16[8,64,512]{2,1,0:T(8,128)(2,1)}, f32[64,4096]{1,0:T(8,128)S(1)}, f32[1,4096]{1,0:T(1,128)S(1)}) custom-call(s32[16]{0:T(128)S(1)} %copy-done.29, bf16[8,192,512]{2,1,0:T(8,128)(2,1)S(1)} %all-to-all-done.qkv_ref), custom_call_target="tpu_custom_call" | custom-call | flops 4294967296 | bytes 2097152 | tf_op jit(solution)/shard_map/attend/pallas_call | solution.py:575
  144.5 12.1 %collective-permute-done.11.refs_3_ = bf16[192,2048]{1,0:T(8,128)(2,1)} collective-permute-done((bf16[192,2048]{1,0:T(8,128)(2,1)}, bf16[192,2048]{1,0:T(8,128)(2,1)}, u32[]{:S(2)}, u32[]{:S(2)}) %collective-permute-start.11) | collective-permute-done | bytes 786464 | tf_op jit(solution)/shard_map/ppermute | solution.py:1297
  168.7 13.6 %collective-permute-done.15 = bf16[2,64,2048]{2,1,0:T(8,128)(2,1)S(1)} collective-permute-done((bf16[2,64,2048]{2,1,0:T(8,128)(2,1)S(1)}, bf16[2,64,2048]{2,1,0:T(8,128)(2,1)S(1)}, u32[]{:S(2)}, u32[]{:S(2)}) %collective-permute-start.15) | collective-permute-done | bytes 524320 | tf_op jit(solution)/shard_map/ppermute | solution.py:1311
  188.2 9.0 %collective-permute-done.13 = bf16[2,64,2048]{2,1,0:T(8,128)(2,1)S(1)} collective-permute-done((bf16[2,64,2048]{2,1,0:T(8,128)(2,1)S(1)}, bf16[2,64,2048]{2,1,0:T(8,128)(2,1)S(1)}, u32[]{:S(2)}, u32[]{:S(2)}) %collective-permute-start.13) | collective-permute-done | bytes 524320 | tf_op jit(solution)/shard_map/ppermute | solution.py:1310
  247.3 8.3 %collective-permute-done.19.refs_2_ = bf16[2,64,2048]{2,1,0:T(8,128)(2,1)S(1)} collective-permute-done((bf16[2,64,2048]{2,1,0:T(8,128)(2,1)S(1)}, bf16[2,64,2048]{2,1,0:T(8,128)(2,1)S(1)}, u32[]{:S(2)}, u32[]{:S(2)}) %collective-permute-start.19) | collective-permute-done | bytes 524320 | tf_op jit(solution)/shard_map/ppermute | solution.py:1279
  264.9 11.2 %collective-permute-done.20.refs_3_ = bf16[2,64,2048]{2,1,0:T(8,128)(2,1)S(1)} collective-permute-done((bf16[2,64,2048]{2,1,0:T(8,128)(2,1)S(1)}, bf16[2,64,2048]{2,1,0:T(8,128)(2,1)S(1)}, u32[]{:S(2)}, u32[]{:S(2)}) %collective-permute-start.20) | collective-permute-done | bytes 524320 | tf_op jit(solution)/shard_map/ppermute | solution.py:1279
  276.9 12.2 %all-gather.5.cloned.1.call-done.refs_14_.w_ref = bf16[4,3,512,2048]{3,2,1,0:T(8,128)(2,1)} async-done(((bf16[4,3,64,2048]{3,2,1,0:T(8,128)(2,1)}), bf16[4,3,512,2048]{3,2,1,0:T(8,128)(2,1)}) %all-gather.5.cloned.1.call-update) | async-done | bytes 25165840 | tf_op jit(solution)/shard_map/all_gather | solution.py:1420
  289.6 33.8 %mlp_forward.1 = (bf16[512,2048]{1,0:T(8,128)(2,1)}, bf16[512,2048]{1,0:T(8,128)(2,1)}, bf16[512,2048]{1,0:T(8,128)(2,1)}, bf16[512,2048]{1,0:T(8,128)(2,1)}, bf...) custom-call(s32[1]{0:T(128)} %bitcast.place_ref, ...), custom_call_target="tpu_custom_call" | custom-call | flops 6871947776 | bytes 11744051 | tf_op jit(solution)/shard_map/mlp_forward/pallas_call | solution.py:989
  326.3 13.6 %gate_up_weights.1 = bf16[8,4,128,2048]{3,2,1,0:T(8,128)(2,1)} custom-call(bf16[512,2048]{1,0:T(8,128)(2,1)} %get-tuple-element.143.x_ref, bf16[512,2048]{1,0:T(8,128)(2,1)} %get-tuple-element.144.gate_ref, bf16[512,2048]{1,0:T(8,128)(2,1)} %get-tuple-element.145.up_ref), custom_call_target="tpu_custom_call" | custom-call | flops 1717986944 | bytes 6710886 | tf_op jit(solution)/shard_map/gate_up_weights/pallas_call | solution.py:1019
  347.9 9.0 %down_weights.1.grads_ref = bf16[8,5,64,2048]{3,2,1,0:T(8,128)(2,1)} custom-call(bf16[512,2048]{1,0:T(8,128)(2,1)} %get-tuple-element.150.u_ref, bf16[512,2048]{1,0:T(8,128)(2,1)} %get-tuple-element.154.hidden_ref), custom_call_target="tpu_custom_call" | custom-call | flops 858993472 | bytes 3355443 | tf_op jit(solution)/shard_map/down_weights/pallas_call | solution.py:1040
  385.3 10.6 %mlp_out.1 = (f32[2,64,2048]{2,1,0:T(8,128)}, bf16[2,64,2048]{2,1,0:T(8,128)(2,1)}, bf16[2,64,2048]{2,1,0:T(8,128)(2,1)}, bf16[2,64,2048]{2,1,0:T(8,128)(2,1)}) custom-call(s32[1]{0:T(128)} %bitcast.place_ref, bf16[512,2048]{1,0:T(8,128)(2,1)} %get-tuple-element.154.hidden_ref, bf16[4,3,512,2048]{3,2,1,0:T(8,128)(2,1)} %all-gather.5.cloned.1.call-done.refs_14_.w_ref), custom_call_target="tpu_custom_call" | custom-call | flops 858993472 | bytes 1677721 | tf_op jit(solution)/shard_map/mlp_out/pallas_call | solution.py:1079
  446.4 27.8 %attend_back.1.refs_10_ = bf16[8,192,512]{2,1,0:T(8,128)(2,1)} custom-call(s32[32]{0:T(128)S(1)} %pad_add_fusion.order_ref, bf16[8,192,512]{2,1,0:T(8,128)(2,1)S(1)} %copy-done.6, bf16[8,64,512]{2,1,0:T(8,128)(2,1)S(1)} %all-to-all-done.2.go_ref, f32[64,4096]{1,0:T(8,128)S(1)} %copy-done.31, f32[1,4096]{1,0:T(1,128)S(1)} %get-tuple-element.175.lse_ref, ...), custom_call_target="tpu_custom_call" | custom-call | flops 6871947776 | bytes 4194304 | tf_op jit(solution)/shard_map/attend_back/pallas_call | solution.py:688
  474.2 9.3 %collective-permute-done.50.refs_6_ = bf16[256,2048]{1,0:T(8,128)(2,1)} collective-permute-done((bf16[256,2048]{1,0:T(8,128)(2,1)}, bf16[256,2048]{1,0:T(8,128)(2,1)}, u32[]{:S(2)}, u32[]{:S(2)}) %collective-permute-start.50) | collective-permute-done | bytes 1048608 | tf_op jit(solution)/shard_map/ppermute | solution.py:1291
  504.4 13.5 %head_weights.1 = bf16[32,64,256]{2,1,0:T(8,128)(2,1)} custom-call(s32[1]{0:T(128)} %bitcast.1.group_ref, bf16[512,2048]{1,0:T(8,128)(2,1)} %get-tuple-element.170.refs_0_, bf16[512,2048]{1,0:T(8,128)(2,1)} %collective-permute-done.47.refs_1_, bf16[512,2048]{1,0:T(8,128)(2,1)} %collective-permute-done.32.refs_2_, ...), custom_call_target="tpu_custom_call" | custom-call | flops 1932735232 | tf_op jit(solution)/shard_map/head_weights/pallas_call | solution.py:1183
  518.6 13.1 %collective-permute-done.55.refs_2_ = bf16[128,2048]{1,0:T(8,128)(2,1)S(1)} collective-permute-done((bf16[128,2048]{1,0:T(8,128)(2,1)S(1)}, bf16[128,2048]{1,0:T(8,128)(2,1)S(1)}, u32[]{:S(2)}, u32[]{:S(2)}) %collective-permute-start.55) | collective-permute-done | bytes 524320 | tf_op jit(solution)/shard_map/ppermute | solution.py:1297
  532.6 8.5 %all-to-all-start.4 = ((bf16[32,64,256]{2,1,0:T(8,128)(2,1)}), bf16[32,64,256]{2,1,0:T(8,128)(2,1)S(1)}, u32[]{:S(2)}, u32[]{:S(2)}) async-start(bf16[32,64,256]{2,1,0:T(8,128)(2,1)} %head_weights.1), calls=%async_computation.5 | async-start | bytes 2097152 | tf_op jit(solution)/shard_map/all_to_all | solution.py:1508
  552.2 22.8 %collective-permute-done.58.refs_3_ = bf16[128,2048]{1,0:T(8,128)(2,1)S(1)} collective-permute-done((bf16[128,2048]{1,0:T(8,128)(2,1)}, bf16[128,2048]{1,0:T(8,128)(2,1)S(1)}, u32[]{:S(2)}, u32[]{:S(2)}) %collective-permute-start.58) | collective-permute-done | bytes 524320 | tf_op jit(solution)/shard_map/ppermute | solution.py:1297
  637.4 16.9 %collective-permute-done.64 = bf16[64,2048]{1,0:T(8,128)(2,1)S(1)} collective-permute-done((bf16[64,2048]{1,0:T(8,128)(2,1)S(1)}, bf16[64,2048]{1,0:T(8,128)(2,1)S(1)}, u32[]{:S(2)}, u32[]{:S(2)}) %collective-permute-start.64) | collective-permute-done | bytes 262176 | tf_op jit(solution)/shard_map/ppermute | solution.py:1527
  (318 shorter events, 324.5 us)
Async XLA Ops:
  7.2 74.0 %all-gather.3.cloned.1.call-start = ((), (), s32[]{:S(2)}) async-start(), calls=%async_computation.7 | async-start | bytes 7077888 | tf_op jit(solution)/shard_map/all_gather | solution.py:1378
  94.2 27.5 %all-to-all-start = ((bf16[8,192,512]{2,1,0:T(8,128)(2,1)}), bf16[8,192,512]{2,1,0:T(8,128)(2,1)S(1)}, u32[]{:S(2)}, u32[]{:S(2)}) async-start(bf16[8,192,512]{2,1,0:T(8,128)(2,1)} %bitcast.6), calls=%async_computation | async-start | bytes 3145728 | tf_op jit(solution)/shard_map/all_to_all | solution.py:1334
  102.1 42.4 %collective-permute-start.10 = (bf16[192,2048]{1,0:T(8,128)(2,1)}, bf16[192,2048]{1,0:T(8,128)(2,1)}, u32[]{:S(2)}, u32[]{:S(2)}) collective-permute-start(bf16[192,2048]{1,0:T(8,128)(2,1)} %get-tuple-element.125), channel_id=1, source_target_pairs={{0,2},{1,3},{2,0},{3,1},{4,6},{5,7},{6,4},{7,5},{8,10},{9,11},{10,... | collective-permute-start | bytes 2359304 | tf_op jit(solution)/shard_map/ppermute | solution.py:1297
  107.3 49.3 %collective-permute-start.11 = (bf16[192,2048]{1,0:T(8,128)(2,1)}, bf16[192,2048]{1,0:T(8,128)(2,1)}, u32[]{:S(2)}, u32[]{:S(2)}) collective-permute-start(bf16[192,2048]{1,0:T(8,128)(2,1)} %get-tuple-element.126), channel_id=1, source_target_pairs={{0,3},{1,0},{2,1},{3,2},{4,7},{5,4},{6,5},{7,6},{8,11},{9,8},{10,9... | collective-permute-start | bytes 2359304 | tf_op jit(solution)/shard_map/ppermute | solution.py:1297
  144.5 144.6 %all-gather.5.cloned.1.call-start = ((), (), s32[]{:S(2)}) async-start(), calls=%async_computation.8 | async-start | bytes 28311552 | tf_op jit(solution)/shard_map/all_gather | solution.py:1420
  161.3 326.5 %reduce-scatter.3.cloned.1.call-start = ((), (), s32[]{:S(2)}) async-start(), calls=%async_computation.9 | async-start | bytes 18874368 | tf_op jit(solution)/shard_map/reduce_scatter | solution.py:1338
  224.1 22.5 %collective-permute-start.28 = (bf16[2,64,2048]{2,1,0:T(8,128)(2,1)S(1)}, bf16[2,64,2048]{2,1,0:T(8,128)(2,1)S(1)}, u32[]{:S(2)}, u32[]{:S(2)}) collective-permute-start(bf16[2,64,2048]{2,1,0:T(8,128)(2,1)S(1)} %collective-permute-done.27.refs_11_), channel_id=1, source_target_pairs={{1,0},{2,1},{5,4},{6,5},{9,8},{10,9},{13,12},{14,13},{17,16},{18,1... | collective-permute-start | bytes 1572872 | tf_op jit(solution)/shard_map/ppermute | solution.py:1280
  235.4 22.5 %collective-permute-start.22 = (bf16[2,64,2048]{2,1,0:T(8,128)(2,1)S(1)}, bf16[2,64,2048]{2,1,0:T(8,128)(2,1)S(1)}, u32[]{:S(2)}, u32[]{:S(2)}) collective-permute-start(bf16[2,64,2048]{2,1,0:T(8,128)(2,1)S(1)} %collective-permute-done.21.refs_4_), channel_id=1, source_target_pairs={{1,0},{2,1},{5,4},{6,5},{9,8},{10,9},{13,12},{14,13},{17,16},{18,1... | collective-permute-start | bytes 1572872 | tf_op jit(solution)/shard_map/ppermute | solution.py:1280
  289.1 50.8 %collective-permute-start.32 = (bf16[512,2048]{1,0:T(8,128)(2,1)}, bf16[512,2048]{1,0:T(8,128)(2,1)}, u32[]{:S(2)}, u32[]{:S(2)}) collective-permute-start(bf16[512,2048]{1,0:T(8,128)(2,1)} %get-tuple-element.170.refs_0_), channel_id=1, source_target_pairs={{0,8},{4,12},{8,0},{12,4},{16,24},{20,28},{24,16},{28,20},{1,9},{5... | collective-permute-start | bytes 6291464 | tf_op jit(solution)/shard_map/ppermute | solution.py:1291
  289.4 50.6 %collective-permute-start.33 = (bf16[512,2048]{1,0:T(8,128)(2,1)}, bf16[512,2048]{1,0:T(8,128)(2,1)}, u32[]{:S(2)}, u32[]{:S(2)}) collective-permute-start(bf16[512,2048]{1,0:T(8,128)(2,1)} %get-tuple-element.170.refs_0_), channel_id=1, source_target_pairs={{0,16},{4,20},{8,24},{12,28},{16,0},{20,4},{24,8},{28,12},{1,17},{... | collective-permute-start | bytes 6291464 | tf_op jit(solution)/shard_map/ppermute | solution.py:1291
  430.3 175.8 %reduce-scatter.5.cloned.1.call-start = ((), (), s32[]{:S(2)}) async-start(), calls=%async_computation.10 | async-start | bytes 11796480 | tf_op jit(solution)/shard_map/reduce_scatter | solution.py:1338
  430.3 53.3 %collective-permute-start.50 = (bf16[256,2048]{1,0:T(8,128)(2,1)}, bf16[256,2048]{1,0:T(8,128)(2,1)}, u32[]{:S(2)}, u32[]{:S(2)}) collective-permute-start(bf16[256,2048]{1,0:T(8,128)(2,1)} %slice.45), channel_id=1, source_target_pairs={{0,16},{4,20},{8,24},{12,28},{16,0},{20,4},{24,8},{28,12},{1,17},{... | collective-permute-start | bytes 3145736 | tf_op jit(solution)/shard_map/ppermute | solution.py:1291
  431.5 52.1 %collective-permute-start.51 = (bf16[256,2048]{1,0:T(8,128)(2,1)}, bf16[256,2048]{1,0:T(8,128)(2,1)}, u32[]{:S(2)}, u32[]{:S(2)}) collective-permute-start(bf16[256,2048]{1,0:T(8,128)(2,1)} %slice.46), channel_id=1, source_target_pairs={{0,8},{4,12},{8,0},{12,4},{16,24},{20,28},{24,16},{28,20},{1,9},{5... | collective-permute-start | bytes 3145736 | tf_op jit(solution)/shard_map/ppermute | solution.py:1291
  437.0 46.6 %collective-permute-start.44 = (bf16[2,64,2048]{2,1,0:T(8,128)(2,1)}, bf16[2,64,2048]{2,1,0:T(8,128)(2,1)}, u32[]{:S(2)}, u32[]{:S(2)}) collective-permute-start(bf16[2,64,2048]{2,1,0:T(8,128)(2,1)} %get-tuple-element.166), channel_id=1, source_target_pairs={{0,1},{1,2},{2,3},{3,0},{4,5},{5,6},{6,7},{7,4},{8,9},{9,10},{10,1... | collective-permute-start | bytes 1572872 | tf_op jit(solution)/shard_map/ppermute | solution.py:1297
  439.3 44.2 %collective-permute-start.45 = (bf16[2,64,2048]{2,1,0:T(8,128)(2,1)}, bf16[2,64,2048]{2,1,0:T(8,128)(2,1)}, u32[]{:S(2)}, u32[]{:S(2)}) collective-permute-start(bf16[2,64,2048]{2,1,0:T(8,128)(2,1)} %get-tuple-element.167), channel_id=1, source_target_pairs={{0,2},{1,3},{2,0},{3,1},{4,6},{5,7},{6,4},{7,5},{8,10},{9,11},{10,... | collective-permute-start | bytes 1572872 | tf_op jit(solution)/shard_map/ppermute | solution.py:1297
  442.9 44.8 %collective-permute-start.46 = (bf16[2,64,2048]{2,1,0:T(8,128)(2,1)}, bf16[2,64,2048]{2,1,0:T(8,128)(2,1)}, u32[]{:S(2)}, u32[]{:S(2)}) collective-permute-start(bf16[2,64,2048]{2,1,0:T(8,128)(2,1)} %get-tuple-element.168), channel_id=1, source_target_pairs={{0,3},{1,0},{2,1},{3,2},{4,7},{5,4},{6,5},{7,6},{8,11},{9,8},{10,9... | collective-permute-start | bytes 1572872 | tf_op jit(solution)/shard_map/ppermute | solution.py:1297
  490.5 42.1 %all-to-all-start.3 = ((bf16[8,192,512]{2,1,0:T(8,128)(2,1)}), bf16[8,192,512]{2,1,0:T(8,128)(2,1)S(1)}, u32[]{:S(2)}, u32[]{:S(2)}) async-start(bf16[8,192,512]{2,1,0:T(8,128)(2,1)} %attend_back.1.refs_10_), calls=%async_computation.4 | async-start | bytes 3145728 | tf_op jit(solution)/shard_map/all_to_all | solution.py:1334
  497.2 34.6 %collective-permute-start.55 = (bf16[128,2048]{1,0:T(8,128)(2,1)S(1)}, bf16[128,2048]{1,0:T(8,128)(2,1)S(1)}, u32[]{:S(2)}, u32[]{:S(2)}) collective-permute-start(bf16[128,2048]{1,0:T(8,128)(2,1)S(1)} %copy-done.58), channel_id=1, source_target_pairs={{0,2},{1,3},{2,0},{3,1},{4,6},{5,7},{6,4},{7,5},{8,10},{9,11},{10,... | collective-permute-start | bytes 1572872 | tf_op jit(solution)/shard_map/ppermute | solution.py:1297
  532.6 50.1 %all-to-all-start.4 = ((bf16[32,64,256]{2,1,0:T(8,128)(2,1)}), bf16[32,64,256]{2,1,0:T(8,128)(2,1)S(1)}, u32[]{:S(2)}, u32[]{:S(2)}) async-start(bf16[32,64,256]{2,1,0:T(8,128)(2,1)} %head_weights.1), calls=%async_computation.5 | async-start | bytes 2097152 | tf_op jit(solution)/shard_map/all_to_all | solution.py:1508
  541.1 33.9 %collective-permute-start.58 = (bf16[128,2048]{1,0:T(8,128)(2,1)}, bf16[128,2048]{1,0:T(8,128)(2,1)S(1)}, u32[]{:S(2)}, u32[]{:S(2)}) collective-permute-start(bf16[128,2048]{1,0:T(8,128)(2,1)} %get-tuple-element.215), channel_id=1, source_target_pairs={{0,3},{1,0},{2,1},{3,2},{4,7},{5,4},{6,5},{7,6},{8,11},{9,8},{10,9... | collective-permute-start | bytes 1572872 | tf_op jit(solution)/shard_map/ppermute | solution.py:1297
  550.1 25.7 %collective-permute-start.56 = (bf16[2,64,2048]{2,1,0:T(8,128)(2,1)S(1)}, bf16[2,64,2048]{2,1,0:T(8,128)(2,1)S(1)}, u32[]{:S(2)}, u32[]{:S(2)}) collective-permute-start(bf16[2,64,2048]{2,1,0:T(8,128)(2,1)S(1)} %get-tuple-element.186), channel_id=1, source_target_pairs={{0,1},{4,5},{8,9},{12,13},{16,17},{20,21},{24,25},{28,29}} | collective-permute-start | bytes 1572872 | tf_op jit(solution)/shard_map/ppermute | solution.py:1310
  550.9 31.7 %collective-permute-start.57 = (bf16[2,64,2048]{2,1,0:T(8,128)(2,1)S(1)}, bf16[2,64,2048]{2,1,0:T(8,128)(2,1)}, u32[]{:S(2)}, u32[]{:S(2)}) collective-permute-start(bf16[2,64,2048]{2,1,0:T(8,128)(2,1)S(1)} %get-tuple-element.184), channel_id=1, source_target_pairs={{3,2},{7,6},{11,10},{15,14},{19,18},{23,22},{27,26},{31,30}} | collective-permute-start | bytes 1572872 | tf_op jit(solution)/shard_map/ppermute | solution.py:1311
  610.4 25.2 %collective-permute-start.66 = (bf16[64,2048]{1,0:T(8,128)(2,1)S(1)}, bf16[64,2048]{1,0:T(8,128)(2,1)S(1)}, u32[]{:S(2)}, u32[]{:S(2)}) collective-permute-start(bf16[64,2048]{1,0:T(8,128)(2,1)S(1)} %get-tuple-element.219), channel_id=1, source_target_pairs={{0,3},{1,0},{2,1},{3,2},{4,7},{5,4},{6,5},{7,6},{8,11},{9,8},{10,9... | collective-permute-start | bytes 786440 | tf_op jit(solution)/shard_map/ppermute | solution.py:1297
  613.8 40.5 %collective-permute-start.64 = (bf16[64,2048]{1,0:T(8,128)(2,1)S(1)}, bf16[64,2048]{1,0:T(8,128)(2,1)S(1)}, u32[]{:S(2)}, u32[]{:S(2)}) collective-permute-start(bf16[64,2048]{1,0:T(8,128)(2,1)S(1)} %slice_bitcast_fusion), channel_id=1, source_target_pairs={{0,0},{1,8},{2,16},{3,24},{4,1},{5,9},{6,17},{7,25},{8,2},{9,10},{... | collective-permute-start | bytes 786440 | tf_op jit(solution)/shard_map/ppermute | solution.py:1527
  (111 other events, 1707.8 us)
Sparse Core Ops, SparseCore 0:
  33.4 47.7 all-gather.2
  161.4 127.6 all-gather.4
  342.7 141.6 reduce-scatter.2
  487.9 94.2 reduce-scatter.4
